TPU v7x, 32 devices: a whole 2x2x4 slice. The times are simulated.
32 devices in a mesh: view: 2 (over y), tile: 16 (over z, x, core).
Axes of the slice: x: 2, y: 2, z: 4, core: 2. Of those that a mesh axis runs over, the one named last changes fastest.
Arguments:
- estimate: float32 [384, 512, 128], P('tile', 'view'), may hold values from 0.5 to 2
- raw_tiles: bfloat16 [4, 384, 512, 128], P('view', 'tile'), may hold values from 0.19921875 to 3
- psf_taps: float32 [4, 3, 17], replicated, may hold values from 0.05 to 1
- view_offsets: int32 [4, 3], replicated, may hold values from -4 to 4, as said below
- depth_range: int32 [4, 16, 2], P(None, 'tile'), may hold values from 0 to 128, as said below
Outputs:
- new_estimate: float32 [384, 512, 128], P('tile', 'view')
Inputs may be any that keep to these rules, and one draw needn't show every extreme that they name: `view_offsets`: some view's offset along the first dimension is 4 and some view's offset along the second dimension is -4. `depth_range`: entry 0 is the first valid depth plane of a view in a raw tile and entry 1 is one past its last; entry 0 < 64 < entry 1.
All inputs are finite; a program needn't handle non-finite values.
Results may differ from a plain program's by a relative error of at most 0.0003.
Values may be sent and summed in bfloat16 or wider, within the bound.
A program may use at most 192 MiB of HBM per device.

v0:
```python
import jax
import jax.numpy as jnp
from jax import lax
from jax.sharding import PartitionSpec as P

HALO = 12


BACKGROUND = 0.1
FLOOR = 0.5
HIGHEST = lax.Precision.HIGHEST


def from_behind(value, axis, steps):
    count = lax.axis_size(axis)
    first, last = (max(0, -steps), min(count, count - steps))
    return lax.ppermute(value, axis, [(source, source + steps) for source in range(first, last)])


def padded(shard, sides, width):
    for axis, dim in sides:
        count, length = (lax.axis_size(axis), shard.shape[dim])
        up = [(i, (i + 1) % count) for i in range(count - 1)]
        down = [(j, i) for i, j in up]
        last = lax.slice_in_dim(shard, length - width, length, axis=dim)
        first = lax.slice_in_dim(shard, 0, width, axis=dim)
        before = lax.ppermute(last, axis, up)
        after = lax.ppermute(first, axis, down)
        shard = jnp.concatenate([before, shard, after], axis=dim)
    return shard


def band_matrix(kernel, offset, rows_in, rows_out, shift):
    taps_count = kernel.shape[0]
    row_index = lax.broadcasted_iota(jnp.int32, (rows_in, rows_out), 0)
    column_index = lax.broadcasted_iota(jnp.int32, (rows_in, rows_out), 1)
    tap_number = row_index - column_index - offset + shift
    tap_range = lax.broadcasted_iota(jnp.int32, (1, 1, taps_count), 2)
    chosen = jnp.where(tap_number[:, :, None] == tap_range, kernel[None, None, :], 0.0)
    return jnp.sum(chosen, axis=2)


def view_setup(
    psf_taps,
    view_offsets,
    depth_range,
    view_id,
    extended,
    block_planes,
    rows_in,
    rows_out,
    row_shift,
    depth_planes,
):
    raw_kernel = psf_taps[view_id]
    kernels = raw_kernel / jnp.sum(raw_kernel, axis=1, keepdims=True)
    offsets = view_offsets[view_id]
    half_taps = raw_kernel.shape[1] // 2
    plane_matrix = band_matrix(kernels[0], offsets[0], extended, block_planes, half_taps - HALO)
    row_matrix = band_matrix(kernels[1], offsets[1], rows_in, rows_out, row_shift)
    depth_matrix = band_matrix(kernels[2], offsets[2], depth_planes, depth_planes, half_taps)
    depth_index = lax.broadcasted_iota(jnp.int32, (depth_planes,), 0)
    inside = (
        (depth_index >= depth_range[view_id, 0, 0]) & (depth_index < depth_range[view_id, 0, 1])
    ).astype(jnp.float32)
    return (plane_matrix, row_matrix, depth_matrix, inside)


def back_project(quotient, plane_matrix, row_matrix, depth_matrix):
    depth_done = jnp.einsum("xyj,ij->xyi", quotient, depth_matrix, precision=HIGHEST)
    rows_done = jnp.einsum("xjz,ij->xiz", depth_done, row_matrix, precision=HIGHEST)
    return jnp.einsum("jyz,ij->iyz", rows_done, plane_matrix, precision=HIGHEST)


def coverage_weight(plane_matrix, row_matrix, depth_matrix, inside):
    plane_sum = jnp.sum(plane_matrix, axis=1)
    row_sum = jnp.sum(row_matrix, axis=1)
    depth_sum = jnp.dot(depth_matrix, inside, precision=HIGHEST)
    return plane_sum[:, None, None] * row_sum[None, :, None] * depth_sum[None, None, :]


def fold_planes(correction, weight):
    block_planes = correction.shape[0] - 2 * HALO
    from_below = from_behind(
        (correction[block_planes + HALO :], weight[block_planes + HALO :]), "tile", 1
    )
    from_above = from_behind((correction[:HALO], weight[:HALO]), "tile", -1)
    folded = []
    for complete, incoming_low, incoming_high in zip((correction, weight), from_below, from_above):
        kept = complete[HALO : block_planes + HALO]
        kept = kept.at[:HALO].add(incoming_low)
        kept = kept.at[block_planes - HALO :].add(incoming_high)
        folded.append(kept)
    return (folded[0], folded[1])


def on_device(estimate, raw_tiles, psf_taps, view_offsets, depth_range):
    block_planes, half_rows, depth_planes = estimate.shape
    extended = block_planes + 2 * HALO
    half_taps = psf_taps.shape[2] // 2
    local_views = raw_tiles.shape[0]
    weight = None
    rows_all = half_rows * lax.axis_size("view")
    view_place = lax.axis_index("view")
    setups = [
        view_setup(
            psf_taps,
            view_offsets,
            depth_range,
            view_place * local_views + view_slot,
            extended,
            block_planes,
            rows_all,
            rows_all,
            half_taps,
            depth_planes,
        )
        for view_slot in range(local_views)
    ]
    margins = padded(estimate.astype(jnp.bfloat16), (("tile", 0),), HALO).astype(estimate.dtype)

    def add_rows(partial_value, shard_rows):
        return tuple(
            (
                partial_value[view_slot]
                + jnp.einsum("xiz,ij->xjz", shard_rows, setups[view_slot][1], precision=HIGHEST)
                for view_slot in range(local_views)
            )
        )

    zeroed = jnp.zeros((extended, rows_all, depth_planes), jnp.float32)
    row_blurred = add_rows(
        tuple((zeroed for view_slot in range(local_views))),
        lax.all_gather(margins.astype(jnp.bfloat16), "view", axis=1, tiled=True).astype(
            jnp.float32
        ),
    )
    correction = jnp.zeros((extended, rows_all, depth_planes), jnp.float32)
    weight = jnp.zeros((extended, rows_all, depth_planes), jnp.float32)
    for view_slot in range(local_views):
        plane_matrix, row_matrix, depth_matrix, inside = setups[view_slot]
        planes_done = jnp.einsum(
            "iyz,ij->jyz", row_blurred[view_slot], plane_matrix, precision=HIGHEST
        )
        predicted = jnp.einsum("xyi,ij->xyj", planes_done, depth_matrix, precision=HIGHEST)
        quotient = inside * raw_tiles[view_slot].astype(jnp.float32) / (predicted + BACKGROUND)
        correction = correction + back_project(quotient, plane_matrix, row_matrix, depth_matrix)
        weight = weight + coverage_weight(plane_matrix, row_matrix, depth_matrix, inside)
    correction, weight = fold_planes(correction, weight)
    correction, weight = (
        lax.psum_scatter(correction, "view", scatter_dimension=1, tiled=True),
        lax.psum_scatter(weight, "view", scatter_dimension=1, tiled=True),
    )
    return (estimate * correction / jnp.maximum(weight, FLOOR)).astype(jnp.float32)


def solution(mesh):
    return jax.shard_map(
        on_device,
        mesh=mesh,
        in_specs=(
            P("tile", "view", None),
            P("view", "tile", None, None),
            P(),
            P(),
            P(None, "tile", None),
        ),
        out_specs=P("tile", "view", None),
        check_vma=False,
    )
```

profile of v0, /device:TPU:1, one launch (start us, length us, event | category | flops | bytes accessed | tf_op | source)
XLA Modules:
  0.0 552.9 jit_solution(2600522305656748421)
XLA Ops:
  12.0 4.5 collective-permute-start
  25.1 3.3 select_reduce_fusion
  28.7 4.4 collective-permute-done
  37.8 5.7 %select_reduce_fusion.2 = (f32[512]{0:T(512)S(1)}, f32[512,512]{1,0:T(8,128)}) fusion(f32[17]{0:T(128)S(1)} %get-tuple-element.74, s32[512,512]{1,0:T(8,128)} %subtract_add_fusion.1), kind=kLoop, calls=%fused_computation.2 | loop fusion | flops 17563136 | bytes 2099268 | tf_op jit(solution)/shard_map/reduce_sum | solution.py:77
  43.7 6.7 %multiply_add_fusion = f32[48,512,128]{2,0,1:T(8,128)S(1)} fusion(f32[128]{0:T(128)S(1)} %convolution_bitcast_fusion.4, f32[48,512]{0,1:T(8,128)S(1)} %broadcast_multiply_fusion, f32[128]{0:T(128)S(1)} %convolution_bitcast_fusion.5, f32[48,512]{0,1:T(8,128)S(1)} %broadcast_multiply_fusion.1), kind=kLoop, calls=%fused_computation.10 | loop fusion | flops 9437184 | bytes 12780544 | tf_op jit(solution)/shard_map/add | solution.py:148
  52.1 4.4 collective-permute-start.4
  67.3 57.0 %collective-permute-done.4 = f32[12,512,128]{2,1,0:T(8,128)S(1)} collective-permute-done((f32[12,512,128]{2,1,0:T(8,128)S(1)}, f32[12,512,128]{2,1,0:T(8,128)S(1)}, u32[]{:S(2)}, u32[]{:S(2)}) %collective-permute-start.4) | collective-permute-done | bytes 3145760 | tf_op jit(solution)/shard_map/ppermute | solution.py:17
  124.4 4.1 slice_add_fusion.1
  128.4 25.2 %scatter-add.16 = f32[24,512,128]{2,0,1:T(8,128)} dynamic-update-slice(f32[24,512,128]{2,0,1:T(8,128)} %slice.203, f32[12,512,128]{2,0,1:T(8,128)} %slice_add_fusion.1, s32[]{:T(128)} %constant.111.clone.1, s32[]{:T(128)} %constant.111.clone.1, s32[]{:T(128)} %constant.111.clone.1) | dynamic-update-slice | bytes 6291460 | tf_op jit(solution)/shard_map/scatter-add | solution.py:91
  153.7 7.2 %slice_add_fusion = f32[12,512,128]{2,0,1:T(8,128)} fusion(f32[24,512,128]{2,0,1:T(8,128)} %scatter-add.16, f32[12,512,128]{2,1,0:T(8,128)} %collective-permute-done.5), kind=kLoop, calls=%fused_computation.30 | loop fusion | flops 786432 | bytes 9437184 | tf_op jit(solution)/shard_map/add | solution.py:92
  160.9 24.6 %scatter-add.19 = f32[24,512,128]{2,0,1:T(8,128)} dynamic-update-slice(f32[24,512,128]{2,0,1:T(8,128)} %scatter-add.16, f32[12,512,128]{2,0,1:T(8,128)} %slice_add_fusion, s32[]{:T(128)} %constant.119.clone.1, s32[]{:T(128)} %constant.111.clone.1, s32[]{:T(128)} %constant.111.clone.1) | dynamic-update-slice | bytes 6291460 | tf_op jit(solution)/shard_map/scatter-add | solution.py:92
  185.6 13.2 %convolution_bitcast_fusion = f32[48,512,128]{2,1,0:T(8,128)S(1)} fusion(bf16[48,512,128]{2,1,0:T(8,128)(2,1)} %all-gather.2.cloned.1.call-done, f32[512,512]{1,0:T(8,128)S(1)} %get-tuple-element.56), kind=kOutput, calls=%fused_computation.27 | convolution fusion | flops 19327352832 | bytes 19922944 | tf_op jit(solution)/shard_map/xiz,ij->xjz/dot_general | solution.py:126
  198.8 14.4 %fusion = f32[24,512,128]{2,0,1:T(8,128)S(1)} fusion(f32[48,512,128]{2,1,0:T(8,128)S(1)} %convolution_bitcast_fusion, f32[48,24]{0,1:T(8,128)S(1)} %get-tuple-element.60), kind=kOutput, calls=%fused_computation.6 | convolution fusion | flops 905969664 | bytes 18878976 | tf_op jit(solution)/shard_map/iyz,ij->jyz/dot_general | solution.py:142
  213.2 5.6 %fusion.12 = f32[24,512,128]{2,1,0:T(8,128)S(1)} fusion(f32[24,512,128]{2,0,1:T(8,128)S(1)} %fusion, f32[128,128]{1,0:T(8,128)S(1)} %select_reduce_fusion.4), kind=kOutput, calls=%fused_computation.19 | convolution fusion | flops 2415919104 | bytes 12648448 | tf_op jit(solution)/shard_map/xyi,ij->xyj/dot_general | solution.py:145
  218.8 11.2 %convolution_bitcast_fusion.1 = f32[48,512,128]{2,1,0:T(8,128)S(1)} fusion(bf16[48,512,128]{2,1,0:T(8,128)(2,1)S(1)} %bitcast.97, f32[512,512]{1,0:T(8,128)S(1)} %copy-done.3), kind=kOutput, calls=%fused_computation.28 | convolution fusion | flops 19327352832 | bytes 19922944 | tf_op jit(solution)/shard_map/xiz,ij->xjz/dot_general | solution.py:126
  230.0 14.3 %fusion.2 = f32[24,512,128]{2,0,1:T(8,128)S(1)} fusion(f32[48,512,128]{2,1,0:T(8,128)S(1)} %convolution_bitcast_fusion.1, f32[48,24]{0,1:T(8,128)S(1)} %get-tuple-element.58), kind=kOutput, calls=%fused_computation.8 | convolution fusion | flops 905969664 | bytes 18878976 | tf_op jit(solution)/shard_map/iyz,ij->jyz/dot_general | solution.py:142
  244.3 5.8 %fusion.16 = f32[24,512,128]{2,1,0:T(8,128)S(1)} fusion(f32[24,512,128]{2,0,1:T(8,128)S(1)} %fusion.2, f32[128,128]{1,0:T(8,128)S(1)} %select_reduce_fusion.5), kind=kOutput, calls=%fused_computation.23 | convolution fusion | flops 2415919104 | bytes 12648448 | tf_op jit(solution)/shard_map/xyi,ij->xyj/dot_general | solution.py:145
  250.2 8.0 %fusion.5 = f32[24,512,128]{2,1,0:T(8,128)S(1)} fusion(f32[24,512,128]{2,1,0:T(8,128)S(1)} %fusion.12, bf16[2,24,512,128]{3,2,1,0:T(8,128)(2,1)} %param.14, f32[128]{0:T(128)S(1)} %fusion.47, f32[128,128]{1,0:T(8,128)S(1)} %select_reduce_fusion.4), kind=kOutput, calls=%fused_computation.13 | convolution fusion | flops 2422210560 | bytes 15794688 | tf_op jit(solution)/shard_map/xyj,ij->xyi/dot_general | solution.py:70
  258.2 11.1 %convolution_bitcast_fusion.2 = f32[24,512,128]{2,1,0:T(8,128)S(1)} fusion(f32[24,512,128]{2,1,0:T(8,128)S(1)} %fusion.5, f32[512,512]{1,0:T(8,128)S(1)} %copy-done.2), kind=kOutput, calls=%fused_computation.45 | convolution fusion | flops 9663676416 | bytes 13631488 | tf_op jit(solution)/shard_map/xjz,ij->xiz/dot_general | solution.py:71
  269.3 6.0 %fusion.8 = f32[24,512,128]{2,1,0:T(8,128)S(1)} fusion(f32[24,512,128]{2,1,0:T(8,128)S(1)} %fusion.16, bf16[2,24,512,128]{3,2,1,0:T(8,128)(2,1)S(1)} %bitcast.99, f32[128]{0:T(128)S(1)} %fusion.46, f32[128,128]{1,0:T(8,128)S(1)} %select_reduce_fusion.5), kind=kOutput, calls=%fused_computation.16 | convolution fusion | flops 2422210560 | bytes 15794688 | tf_op jit(solution)/shard_map/xyj,ij->xyi/dot_general | solution.py:70
  275.3 11.1 %convolution_bitcast_fusion.3 = f32[24,512,128]{2,1,0:T(8,128)S(1)} fusion(f32[24,512,128]{2,1,0:T(8,128)S(1)} %fusion.8, f32[512,512]{1,0:T(8,128)S(1)} %copy-done.4), kind=kOutput, calls=%fused_computation.46 | convolution fusion | flops 9663676416 | bytes 13631488 | tf_op jit(solution)/shard_map/xjz,ij->xiz/dot_general | solution.py:71
  286.3 14.6 %fusion.10 = f32[48,512,128]{2,0,1:T(8,128)S(1)} fusion(f32[24,512,128]{2,1,0:T(8,128)S(1)} %convolution_bitcast_fusion.2, f32[48,24]{0,1:T(8,128)S(1)} %get-tuple-element.60), kind=kOutput, calls=%fused_computation.17 | convolution fusion | flops 905969664 | bytes 18878976 | tf_op jit(solution)/shard_map/jyz,ij->iyz/dot_general | solution.py:72
  301.0 20.1 %fusion.20 = f32[48,512,128]{2,0,1:T(8,128)} fusion(f32[48,512,128]{2,0,1:T(8,128)S(1)} %fusion.10, f32[24,512,128]{2,1,0:T(8,128)S(1)} %convolution_bitcast_fusion.3, f32[48,24]{0,1:T(8,128)S(1)} %get-tuple-element.58), kind=kOutput, calls=%fused_computation.29 | convolution fusion | flops 909115392 | bytes 31461888 | tf_op jit(solution)/shard_map/jyz,ij->iyz/dot_general | solution.py:72
  321.1 4.3 fusion.53
  328.0 4.5 collective-permute-start.2
  338.9 61.8 %collective-permute-done.2 = f32[12,512,128]{2,1,0:T(8,128)S(1)} collective-permute-done((f32[12,512,128]{2,1,0:T(8,128)}, f32[12,512,128]{2,1,0:T(8,128)S(1)}, u32[]{:S(2)}, u32[]{:S(2)}) %collective-permute-start.2) | collective-permute-done | bytes 3145760 | tf_op jit(solution)/shard_map/ppermute | solution.py:17
  400.7 4.1 slice_add_fusion.3
  404.8 25.3 %scatter-add.14 = f32[24,512,128]{2,0,1:T(8,128)} dynamic-update-slice(f32[24,512,128]{2,0,1:T(8,128)} %slice.198, f32[12,512,128]{2,0,1:T(8,128)} %slice_add_fusion.3, s32[]{:T(128)} %constant.111.clone.1, s32[]{:T(128)} %constant.111.clone.1, s32[]{:T(128)} %constant.111.clone.1) | dynamic-update-slice | bytes 6291460 | tf_op jit(solution)/shard_map/scatter-add | solution.py:91
  430.0 7.2 %slice_add_fusion.2 = f32[12,512,128]{2,0,1:T(8,128)} fusion(f32[24,512,128]{2,0,1:T(8,128)} %scatter-add.14, f32[12,512,128]{2,1,0:T(8,128)} %collective-permute-done.3), kind=kLoop, calls=%fused_computation.32 | loop fusion | flops 786432 | bytes 9437184 | tf_op jit(solution)/shard_map/add | solution.py:92
  437.3 24.8 %scatter-add.15 = f32[24,512,128]{2,0,1:T(8,128)} dynamic-update-slice(f32[24,512,128]{2,0,1:T(8,128)} %scatter-add.14, f32[12,512,128]{2,0,1:T(8,128)} %slice_add_fusion.2, s32[]{:T(128)} %constant.119.clone.1, s32[]{:T(128)} %constant.111.clone.1, s32[]{:T(128)} %constant.111.clone.1) | dynamic-update-slice | bytes 6291460 | tf_op jit(solution)/shard_map/scatter-add | solution.py:92
  462.1 77.0 %reduce-scatter.3.cloned.1.call-done = f32[24,256,128]{2,0,1:T(8,128)} async-done(((f32[24,512,128]{2,0,1:T(8,128)}), f32[24,256,128]{2,0,1:T(8,128)}) %reduce-scatter.3.cloned.1.call-update) | async-done | bytes 3145744 | tf_op jit(solution)/shard_map/reduce_scatter | solution.py:151
  539.1 4.8 fusion.25
  (81 shorter events, 43.0 us)
Async XLA Ops:
  6.5 9.9 %copy-start.6 = (f32[4,3,17]{2,0,1:T(4,128)S(1)}, f32[4,3,17]{2,0,1:T(4,128)}, u32[]{:S(2)}) copy-start(f32[4,3,17]{2,0,1:T(4,128)} %param.15) | copy-start | bytes 2452
  6.5 10.1 %copy-start.7 = (s32[4,3]{1,0:T(4,128)S(1)}, s32[4,3]{1,0:T(4,128)}, u32[]{:S(2)}) copy-start(s32[4,3]{1,0:T(4,128)} %param.16) | copy-start | bytes 148
  6.5 12.8 %copy-start.5 = (s32[4,1,2]{0,2,1:T(2,128)S(1)}, s32[4,1,2]{0,2,1:T(2,128)}, u32[]{:S(2)}) copy-start(s32[4,1,2]{0,2,1:T(2,128)} %param.17) | copy-start | bytes 100
  6.5 179.1 %all-gather.2.cloned.1.call-start = ((), (), s32[]{:S(2)}) async-start(), calls=%async_computation.2 | async-start | bytes 9437184 | tf_op jit(solution)/shard_map/all_gather | solution.py:134
  10.0 18.6 %collective-permute-start.1 = (bf16[12,256,128]{2,1,0:T(8,128)(2,1)}, bf16[12,256,128]{2,1,0:T(8,128)(2,1)}, u32[]{:S(2)}, u32[]{:S(2)}) collective-permute-start(bf16[12,256,128]{2,1,0:T(8,128)(2,1)} %get-tuple-element.70), channel_id=1, source_target_pairs={{1,0},{2,1},{3,2},{4,3},{5,4},{6,5},{7,6},{8,7},{9,8},{10,9},{11,1... | collective-permute-start | bytes 2359304 | tf_op jit(solution)/shard_map/ppermute | solution.py:28
  12.0 21.1 %collective-permute-start = (bf16[12,256,128]{2,1,0:T(8,128)(2,1)}, bf16[12,256,128]{2,1,0:T(8,128)(2,1)}, u32[]{:S(2)}, u32[]{:S(2)}) collective-permute-start(bf16[12,256,128]{2,1,0:T(8,128)(2,1)} %get-tuple-element.69), channel_id=1, source_target_pairs={{0,1},{1,2},{2,3},{3,4},{4,5},{5,6},{6,7},{7,8},{8,9},{9,10},{10,1... | collective-permute-start | bytes 2359304 | tf_op jit(solution)/shard_map/ppermute | solution.py:27
  28.5 157.1 %copy-start.1 = (f32[512,512]{1,0:T(8,128)}, f32[512,512]{1,0:T(8,128)S(1)}, u32[]{:S(2)}) copy-start(f32[512,512]{1,0:T(8,128)S(1)} %get-tuple-element.56) | copy-start | bytes 3145732
  36.1 426.0 %reduce-scatter.5.cloned.1.call-start = ((), (), s32[]{:S(2)}) async-start(), calls=%async_computation.4 | async-start | bytes 9437184 | tf_op jit(solution)/shard_map/reduce_scatter | solution.py:152
  52.1 72.3 %collective-permute-start.4 = (f32[12,512,128]{2,1,0:T(8,128)S(1)}, f32[12,512,128]{2,1,0:T(8,128)S(1)}, u32[]{:S(2)}, u32[]{:S(2)}) collective-permute-start(f32[12,512,128]{2,1,0:T(8,128)S(1)} %copy.41), channel_id=1, source_target_pairs={{0,1},{1,2},{2,3},{3,4},{4,5},{5,6},{6,7},{7,8},{8,9},{9,10},{10,1... | collective-permute-start | bytes 9437192 | tf_op jit(solution)/shard_map/ppermute | solution.py:17
  59.1 94.6 %collective-permute-start.5 = (f32[12,512,128]{2,1,0:T(8,128)}, f32[12,512,128]{2,1,0:T(8,128)}, u32[]{:S(2)}, u32[]{:S(2)}) collective-permute-start(f32[12,512,128]{2,1,0:T(8,128)} %copy.43), channel_id=1, source_target_pairs={{1,0},{2,1},{3,2},{4,3},{5,4},{6,5},{7,6},{8,7},{9,8},{10,9},{11,1... | collective-permute-start | bytes 9437192 | tf_op jit(solution)/shard_map/ppermute | solution.py:17
  185.5 353.6 %reduce-scatter.3.cloned.1.call-start = ((), (), s32[]{:S(2)}) async-start(), calls=%async_computation.3 | async-start | bytes 9437184 | tf_op jit(solution)/shard_map/reduce_scatter | solution.py:151
  198.8 20.0 %slice-start.3 = ((s8[6291456]{0:T(1024)(128)(4,1)}), s8[4194304]{0:T(1024)(128)(4,1)S(1)}, s32[]{:S(2)}) async-start(s8[6291456]{0:T(1024)(128)(4,1)} %bitcast.96), calls=%async_computation.8 | async-start | bytes 8388608
  213.2 5.6 %slice-start.4 = ((s8[6291456]{0:T(1024)(128)(4,1)}), s8[2097152]{0:T(1024)(128)(4,1)S(1)}, s32[]{:S(2)}) async-start(s8[6291456]{0:T(1024)(128)(4,1)} %bitcast.96), calls=%async_computation.9 | async-start | bytes 4194304
  213.2 5.6 %copy-start.3 = (f32[512,512]{1,0:T(8,128)S(1)}, f32[512,512]{1,0:T(8,128)}, u32[]{:S(2)}) copy-start(f32[512,512]{1,0:T(8,128)} %get-tuple-element.54) | copy-start | bytes 3145732
  244.3 24.9 %slice-start.5 = ((s8[6291456]{0:T(1024)(128)(4,1)}), s8[4194304]{0:T(1024)(128)(4,1)S(1)}, s32[]{:S(2)}) async-start(s8[6291456]{0:T(1024)(128)(4,1)} %bitcast.98), calls=%async_computation.10 | async-start | bytes 8388608
  250.1 8.0 %copy-start.2 = (f32[512,512]{1,0:T(8,128)S(1)}, f32[512,512]{1,0:T(8,128)}, u32[]{:S(2)}) copy-start(f32[512,512]{1,0:T(8,128)} %copy-done.1) | copy-start | bytes 3145732
  250.1 19.1 %slice-start.6 = ((s8[6291456]{0:T(1024)(128)(4,1)}), s8[2097152]{0:T(1024)(128)(4,1)S(1)}, s32[]{:S(2)}) async-start(s8[6291456]{0:T(1024)(128)(4,1)} %bitcast.98), calls=%async_computation.11 | async-start | bytes 4194304
  269.3 6.0 %copy-start.4 = (f32[512,512]{1,0:T(8,128)S(1)}, f32[512,512]{1,0:T(8,128)}, u32[]{:S(2)}) copy-start(f32[512,512]{1,0:T(8,128)} %get-tuple-element.54) | copy-start | bytes 3145732
  321.1 14.6 %slice-start = ((s8[12582912]{0:T(1024)(128)(4,1)}), s8[4194304]{0:T(1024)(128)(4,1)S(1)}, s32[]{:S(2)}) async-start(s8[12582912]{0:T(1024)(128)(4,1)} %bitcast.94), calls=%async_computation.5 | async-start | bytes 8388608
  321.1 14.6 %slice-start.1 = ((s8[12582912]{0:T(1024)(128)(4,1)}), s8[4194304]{0:T(1024)(128)(4,1)S(1)}, s32[]{:S(2)}) async-start(s8[12582912]{0:T(1024)(128)(4,1)} %bitcast.94), calls=%async_computation.6 | async-start | bytes 8388608
  325.3 10.3 %slice-start.2 = ((s8[12582912]{0:T(1024)(128)(4,1)}), s8[4194304]{0:T(1024)(128)(4,1)S(1)}, s32[]{:S(2)}) async-start(s8[12582912]{0:T(1024)(128)(4,1)} %bitcast.94), calls=%async_computation.7 | async-start | bytes 8388608
  328.0 72.7 %collective-permute-start.2 = (f32[12,512,128]{2,1,0:T(8,128)}, f32[12,512,128]{2,1,0:T(8,128)S(1)}, u32[]{:S(2)}, u32[]{:S(2)}) collective-permute-start(f32[12,512,128]{2,1,0:T(8,128)} %copy.36), channel_id=1, source_target_pairs={{0,1},{1,2},{2,3},{3,4},{4,5},{5,6},{6,7},{7,8},{8,9},{9,10},{10,1... | collective-permute-start | bytes 9437192 | tf_op jit(solution)/shard_map/ppermute | solution.py:17
  333.5 96.5 %collective-permute-start.3 = (f32[12,512,128]{2,1,0:T(8,128)S(1)}, f32[12,512,128]{2,1,0:T(8,128)}, u32[]{:S(2)}, u32[]{:S(2)}) collective-permute-start(f32[12,512,128]{2,1,0:T(8,128)S(1)} %copy.38), channel_id=1, source_target_pairs={{1,0},{2,1},{3,2},{4,3},{5,4},{6,5},{7,6},{8,7},{9,8},{10,9},{11,1... | collective-permute-start | bytes 9437192 | tf_op jit(solution)/shard_map/ppermute | solution.py:17
  437.3 101.8 %copy-start = (f32[24,256,128]{2,1,0:T(8,128)S(1)}, f32[24,256,128]{2,1,0:T(8,128)}, u32[]{:S(2)}) copy-start(f32[24,256,128]{2,1,0:T(8,128)} %param.13) | copy-start | bytes 9437188
Sparse Core Ops, SparseCore 0:
  36.2 81.3 all-gather.1
  185.7 77.9 reduce-scatter.4
  462.2 76.8 reduce-scatter.2
where the time goes:
time: 560 us; the launch traced here: 553 us
  waiting for transfers between devices  200 us (36%)
  matrix products  138 us (25%)
  local copies, waits for them, and re-layouts  123 us (22%)
  other arithmetic  57 us (10%)
  starting transfers between devices  20.2 us (4%)
  between operations  13.8 us (2%)
    ppermute x4, waiting for transfers between devices, from_behind(): lax.ppermute(value, axis, [(source, source + steps) for source in range(f...  119 us
    reduce_scatter x1, waiting for transfers between devices, on_device(): lax.psum_scatter(correction, 'view', scatter_dimension=1, tiled=True)  77 us
    scatter-add x2, local copies, waits for them, and re-layouts, fold_planes(): kept = kept.at[:HALO].add(incoming_low)  50.5 us
    scatter-add x2, local copies, waits for them, and re-layouts, fold_planes(): kept = kept.at[block_planes - HALO:].add(incoming_high)  49.4 us
    dot_general x2, matrix products, back_project(): return jnp.einsum('jyz,ij->iyz', rows_done, plane_matrix, precision=HIGHEST)  34.7 us
    dot_general x2, matrix products, on_device(): jnp.einsum('iyz,ij->jyz', row_blurred[view_slot], plane_matrix, precision...  28.7 us
    dot_general x2, matrix products, add_rows(): jnp.einsum('xiz,ij->xjz', shard_rows, setups[view_slot][1], precision=HIG...  24.3 us
    dot_general x2, matrix products, back_project(): jnp.einsum('xjz,ij->xiz', depth_done, row_matrix, precision=HIGHEST)  22.1 us
  transfers between devices with their start and end apart: 9, of which 4 were waited for; matrix products, arithmetic and copies ran while one was open for 55% of the time, Pallas kernels for 0%

commit v1 on v0

v1 whole, which is shorter than its diff:
```python
import functools

import jax
import jax.numpy as jnp
from jax import lax
from jax.experimental import pallas as pl
from jax.experimental.pallas import tpu as pltpu
from jax.sharding import PartitionSpec as P

MAXOFF = 4
BACKGROUND = 0.1
FLOOR = 0.5
EST_MID = 1.25
QUO_MID = 1.1875
SUB = 8
ROWS = 16
PLANES = 4
F32 = jnp.float32
BF16 = jnp.bfloat16
VMEM_LIMIT = 48 * 1024 * 1024


def tap_lookup(kernel, number):
    total = jnp.zeros(number.shape, kernel.dtype)
    for tap in range(kernel.shape[1]):
        value = kernel[:, tap].reshape((-1,) + (1,) * (number.ndim - 1))
        total = jnp.where(number == tap, value, total)
    return total


def rows_forward_kernel(est_ref, matrix_ref, out_ref):
    views, planes, rows, depth = out_ref.shape
    for pair in range(0, planes, 2):
        data = jnp.concatenate([est_ref[pair], est_ref[pair + 1]], axis=1)
        done = jnp.dot(matrix_ref[...], data, preferred_element_type=F32)
        for view in range(views):
            part = done[view * rows : (view + 1) * rows].astype(out_ref.dtype)
            out_ref[view, pair] = part[:, :depth]
            out_ref[view, pair + 1] = part[:, depth:]


def rows_forward(est, matrix, views):
    count, rows_in, depth = est.shape
    rows = matrix.shape[0] // views
    return pl.pallas_call(
        rows_forward_kernel,
        grid=(count // PLANES,),
        in_specs=[
            pl.BlockSpec((PLANES, rows_in, depth), lambda i: (i, 0, 0)),
            pl.BlockSpec(matrix.shape, lambda i: (0, 0)),
        ],
        out_specs=pl.BlockSpec((views, PLANES, rows, depth), lambda i: (0, i, 0, 0)),
        out_shape=jax.ShapeDtypeStruct((views, count, rows, depth), BF16),
        compiler_params=pltpu.CompilerParams(vmem_limit_bytes=VMEM_LIMIT),
        cost_estimate=pl.CostEstimate(
            flops=2 * count * depth * rows_in * views * rows,
            bytes_accessed=2 * (est.size + views * count * rows * depth),
            transcendentals=0,
        ),
    )(est, matrix)


def view_kernel(
    scalar_ref,
    inner_ref,
    outer_ref,
    raw_ref,
    plane_ref,
    plane_t_ref,
    depth_ref,
    depth_t_ref,
    ones_x_ref,
    ones_yz_ref,
    cover_ref,
    scale_ref,
    out_ref,
    ext_ref,
):
    block, _, depth = raw_ref.shape
    halo = outer_ref.shape[0] // 2
    window = plane_ref.shape[1] // SUB
    start = scalar_ref[0]
    ext_ref[:halo] = outer_ref[:halo]
    ext_ref[halo : halo + block] = inner_ref[...]
    ext_ref[halo + block :] = outer_ref[halo:]
    source = ext_ref[pl.ds(start, window)].astype(F32)
    halves = [
        source[:, lo : lo + SUB].reshape(window * SUB, depth) for lo in range(0, ROWS, SUB)
    ]
    data = jnp.concatenate(halves, axis=1).astype(BF16)
    planes = jnp.dot(plane_ref[...], data, preferred_element_type=F32)
    stacked = jnp.concatenate([planes[:, :depth], planes[:, depth:]], axis=0).astype(BF16)
    blurred = jnp.dot(stacked, depth_ref[...], preferred_element_type=F32)
    blurred = blurred.reshape(2, block, SUB, depth)
    raw = raw_ref[...].astype(F32)
    scale = scale_ref[...]
    cover = cover_ref[...] * scale
    ones_x = ones_x_ref[...]
    quotients = []
    for half in range(2):
        ones_yz = ones_yz_ref[half * SUB : (half + 1) * SUB]
        predicted = blurred[half] * scale + ones_x * ones_yz
        ratio = raw[:, half * SUB : (half + 1) * SUB] / (predicted + BACKGROUND)
        quotients.append((cover * (ratio - QUO_MID)).reshape(block * SUB, depth))
    quotient = jnp.concatenate(quotients, axis=0).astype(BF16)
    back = jnp.dot(quotient, depth_t_ref[...], preferred_element_type=F32)
    size = block * SUB
    back = jnp.concatenate([back[:size], back[size:]], axis=1).astype(BF16)
    spread = jnp.dot(plane_t_ref[...], back, preferred_element_type=F32)
    spread = [
        spread[:, lo : lo + depth].reshape(window, SUB, depth) for lo in (0, depth)
    ]
    out_ref[...] = jnp.zeros_like(out_ref)
    out_ref[pl.ds(start, window)] = jnp.concatenate(spread, axis=1).astype(out_ref.dtype)


def view_pass(view, slot, base, start, inner, outer, raw, tables):
    _, block, rows, depth = inner.shape
    halo2 = outer.shape[1]
    plane, plane_t, depth_m, depth_mt, ones_x, ones_yz, cover, scale = tables
    scalars = jnp.stack([start, base]).astype(jnp.int32)

    def table(array):
        zeros = (0,) * (array.ndim - 1)
        return pl.BlockSpec((None,) + array.shape[1:], lambda g, s: (view,) + zeros)

    rows_block = pl.BlockSpec((None, block, ROWS, depth), lambda g, s: (view, 0, g, 0))
    outer_block = pl.BlockSpec((None, halo2, ROWS, depth), lambda g, s: (view, 0, g, 0))
    return pl.pallas_call(
        view_kernel,
        grid_spec=pltpu.PrefetchScalarGridSpec(
            num_scalar_prefetch=1,
            grid=(rows // ROWS,),
            in_specs=[
                rows_block,
                outer_block,
                pl.BlockSpec((None, block, ROWS, depth), lambda g, s: (slot, 0, s[1] + g, 0)),
                table(plane),
                table(plane_t),
                table(depth_m),
                table(depth_mt),
                table(ones_x),
                pl.BlockSpec((None, ROWS, depth), lambda g, s: (view, g, 0)),
                table(cover),
                table(scale),
            ],
            out_specs=pl.BlockSpec((block + halo2, ROWS, depth), lambda g, s: (0, g, 0)),
            scratch_shapes=[pltpu.VMEM((block + halo2, ROWS, depth), BF16)],
        ),
        out_shape=jax.ShapeDtypeStruct((block + halo2, rows, depth), BF16),
        compiler_params=pltpu.CompilerParams(vmem_limit_bytes=VMEM_LIMIT),
        cost_estimate=pl.CostEstimate(
            flops=2 * (rows // ROWS) * 2_000 * 256 * 256,
            bytes_accessed=2 * rows * depth * (5 * block),
            transcendentals=block * rows * depth,
        ),
    )(
        scalars,
        inner,
        outer,
        raw,
        plane,
        plane_t,
        depth_m,
        depth_mt,
        ones_x,
        ones_yz,
        cover,
        scale,
    )


def rows_back_kernel(*refs):
    *part_refs, matrix_ref, out_ref = refs
    planes, _, depth = out_ref.shape
    for pair in range(0, planes, 2):
        data = jnp.concatenate(
            [jnp.concatenate([ref[pair], ref[pair + 1]], axis=1) for ref in part_refs], axis=0
        )
        done = jnp.dot(matrix_ref[...], data, preferred_element_type=F32).astype(out_ref.dtype)
        out_ref[pair] = done[:, :depth]
        out_ref[pair + 1] = done[:, depth:]


def rows_back(parts, matrix, blocks, place, dtype):
    _, rows, depth = parts[0].shape
    rows_out = matrix.shape[0]
    return pl.pallas_call(
        rows_back_kernel,
        grid=(blocks,),
        in_specs=[pl.BlockSpec((PLANES, rows, depth), lambda i: (place(i), 0, 0)) for _ in parts]
        + [pl.BlockSpec(matrix.shape, lambda i: (0, 0))],
        out_specs=pl.BlockSpec((PLANES, rows_out, depth), lambda i: (i, 0, 0)),
        out_shape=jax.ShapeDtypeStruct((blocks * PLANES, rows_out, depth), dtype),
        compiler_params=pltpu.CompilerParams(vmem_limit_bytes=VMEM_LIMIT),
        cost_estimate=pl.CostEstimate(
            flops=2 * blocks * PLANES * depth * matrix.size,
            bytes_accessed=2 * blocks * PLANES * depth * (len(parts) * rows + 2 * rows_out),
            transcendentals=0,
        ),
    )(*parts, matrix)


def on_device(estimate, raw_tiles, psf_taps, view_offsets, depth_range):
    block, half_rows, depth = estimate.shape
    slots = raw_tiles.shape[0]
    views, _, taps = psf_taps.shape
    half = taps // 2
    halo = half + MAXOFF
    tiles = lax.axis_size("tile")
    tile = lax.axis_index("tile")
    place = lax.axis_index("view")
    planes_all = block * tiles
    rows_all = half_rows * lax.axis_size("view")
    swap = [(0, 1), (1, 0)]
    up = [(i, i + 1) for i in range(tiles - 1)]
    down = [(i + 1, i) for i in range(tiles - 1)]
    quo_rows = half_rows + ROWS
    est_extra = 2 * ROWS
    iota = functools.partial(lax.broadcasted_iota, jnp.int32)

    centred = (estimate - EST_MID).astype(BF16)
    edge = lax.dynamic_slice_in_dim(centred, (1 - place) * (half_rows - est_extra), est_extra, 1)
    inner_est = jnp.concatenate([centred, lax.ppermute(edge, "view", swap)], axis=1)
    outer_est = jnp.concatenate(
        [
            lax.ppermute(inner_est[block - halo :], "tile", up),
            lax.ppermute(inner_est[:halo], "tile", down),
        ],
        axis=0,
    )

    other_start = (1 - place) * (half_rows - ROWS)
    arrived = []
    for slot in range(slots):
        piece = lax.dynamic_slice_in_dim(raw_tiles[slot], other_start, quo_rows, 1)
        arrived.append(lax.ppermute(piece, "view", swap)[None])

    def own_first(array):
        return jnp.where(place == 0, array, jnp.roll(array, slots, axis=0))

    raw_taps = own_first(psf_taps)
    offsets = own_first(view_offsets)
    kernels = raw_taps / jnp.sum(raw_taps, axis=2, keepdims=True)
    rounded = kernels.astype(BF16).astype(F32)
    scale = 1.0 / jnp.prod(jnp.sum(rounded, axis=2), axis=1)
    limits = jnp.stack(
        [
            lax.ppermute(depth_range, "tile", up),
            depth_range,
            lax.ppermute(depth_range, "tile", down),
        ]
    )
    limits = own_first(limits[:, :, 0].transpose(1, 0, 2))
    depth_index = jnp.arange(depth)
    cover3 = (
        (depth_index >= limits[:, :, :1]) & (depth_index < limits[:, :, 1:])
    ).astype(F32)

    ox, oy, oz = (offsets[:, dim] for dim in range(3))
    window = block + taps - 1

    shape = (views, block * SUB, window * SUB)
    row, column = iota(shape, 1), iota(shape, 2)
    step = jnp.where(row % SUB == column % SUB, column // SUB - row // SUB, -1)
    plane_m = tap_lookup(rounded[:, 0], step).astype(BF16)
    plane_mt = plane_m.transpose(0, 2, 1)

    shape = (views, depth, depth)
    depth_m = tap_lookup(
        rounded[:, 2], iota(shape, 1) - iota(shape, 2) - oz[:, None, None] + half
    ).astype(BF16)
    depth_mt = depth_m.transpose(0, 2, 1)

    quo_first = place * (half_rows - ROWS)
    shape = (views, quo_rows, half_rows + est_extra)
    position = iota(shape, 2)
    from_row = jnp.where(
        position < half_rows,
        place * half_rows + position,
        (1 - place) * half_rows + place * (half_rows - est_extra) + position - half_rows,
    )
    to_row = quo_first + iota(shape, 1)
    rows_m = tap_lookup(rounded[:, 1], from_row - to_row - oy[:, None, None] + half)
    rows_m = rows_m.astype(BF16).reshape(views * quo_rows, half_rows + est_extra)

    shape = (views, half_rows, quo_rows)
    to_row = place * half_rows + iota(shape, 1)
    from_row = quo_first + iota(shape, 2)
    rows_mt = tap_lookup(rounded[:, 1], to_row - from_row - oy[:, None, None] + half)
    rows_mt = rows_mt.astype(BF16).transpose(1, 0, 2).reshape(half_rows, views * quo_rows)

    tap = jnp.arange(taps)

    def inside_sum(kernel, index, count):
        inside = (index >= 0) & (index < count)
        return jnp.sum(jnp.where(inside, kernel[:, None, :], 0.0), axis=2)

    def reached(first, count, offset, direction):
        base = first + jnp.arange(count)
        return base[None, :, None] + direction * (offset[:, None, None] + tap - half)

    ones_x = inside_sum(kernels[:, 0], reached(tile * block, block, ox, 1), planes_all)
    ones_y = inside_sum(kernels[:, 1], reached(quo_first, quo_rows, oy, 1), rows_all)
    ones_z = inside_sum(kernels[:, 2], reached(0, depth, oz, 1), depth)
    ones_yz = EST_MID * ones_y[:, :, None] * ones_z[:, None, :]
    ones_x = jnp.broadcast_to(ones_x[:, :, None, None], (views, block, SUB, depth))
    cover = jnp.broadcast_to(cover3[:, 1][:, None, :], (views, SUB, depth))
    scales = jnp.broadcast_to(scale[:, None, None], (views, SUB, depth))
    tables = (plane_m, plane_mt, depth_m, depth_mt, ones_x, ones_yz, cover, scales)

    taken = jnp.einsum(
        "wkj,wij->wki",
        cover3,
        tap_lookup(
            kernels[:, 2],
            iota((views, depth, depth), 1) - iota((views, depth, depth), 2)
            - oz[:, None, None]
            + half,
        ),
        precision=lax.Precision.HIGHEST,
    )
    from_plane = reached(0, block, ox, -1)
    table_xz = 0.0
    for side in range(3):
        low = (side - 1) * block
        share = inside_sum(kernels[:, 0], from_plane - low, block)
        table_xz = table_xz + share[:, :, None] * taken[:, side][:, None, :]
    back_y = inside_sum(
        kernels[:, 1], reached(place * half_rows, half_rows, oy, -1), rows_all
    )

    inner = rows_forward(inner_est, rows_m, views)
    outer = rows_forward(outer_est, rows_m, views)
    starts = ox + (halo - half)
    parts = []
    for view in range(views):
        mine = view < slots
        parts.append(
            view_pass(
                view,
                view if mine else 0,
                place * ((half_rows - ROWS) // ROWS) if mine else jnp.int32(0),
                starts[view],
                inner,
                outer,
                raw_tiles if mine else arrived[view - slots],
                tables,
            )
        )

    side = halo // PLANES
    middle = block // PLANES
    edges = rows_back(
        parts, rows_mt, 2 * side, lambda i: jnp.where(i < side, i, i + middle), BF16
    )
    kept = rows_back(parts, rows_mt, middle, lambda i: i + side, F32)
    low = lax.ppermute(edges[halo:], "tile", up)
    high = lax.ppermute(edges[:halo], "tile", down)
    low = jnp.pad(low, ((0, block - halo), (0, 0), (0, 0)))
    high = jnp.pad(high, ((block - halo, 0), (0, 0), (0, 0)))
    weight = sum(
        table_xz[view][:, None, :] * back_y[view][None, :, None] for view in range(views)
    )
    correction = kept + low.astype(F32) + high.astype(F32) + QUO_MID * weight
    return estimate * correction / jnp.maximum(weight, FLOOR)


def solution(mesh):
    return jax.shard_map(
        on_device,
        mesh=mesh,
        in_specs=(
            P("tile", "view", None),
            P("view", "tile", None, None),
            P(),
            P(),
            P(None, "tile", None),
        ),
        out_specs=P("tile", "view", None),
        check_vma=False,
    )
```

time: 560 us -> 181 us (0.32)
  waiting for transfers between devices: 200 us -> 17.8 us
  matrix products: 138 us -> 0.67 us
  local copies, waits for them, and re-layouts: 123 us -> 21.8 us
  Pallas kernels: 0 us -> 92.9 us
  other arithmetic: 57 us -> 21.5 us
  between operations: 13.8 us -> 0.99 us
    dot_general x14 -> x1, matrix products: 138 us -> 0.67 us  [on_device(): jnp.einsum('wkj,wij->wki', cover3, tap_lookup(kernels[:, 2], iota((views,...]
    ppermute x6 -> x9, waiting for transfers between devices: 123 us -> 17.8 us  [the longest x1 9.23 us: on_device(): low = lax.ppermute(edges[halo:], 'tile', up)]
    scatter-add x4 -> x0, local copies, waits for them, and re-layouts: 99.9 us -> none  [the longest x2 50.5 us: fold_planes(): kept = kept.at[:HALO].add(incoming_low)]
    pallas_call x0 -> x8, Pallas kernels: none -> 92.9 us  [the longest x4 69.2 us: view_pass(): pl.pallas_call(view_kernel, grid_spec=pltpu.PrefetchScalarGridSpec(num_sc...]
    reduce_scatter x2 -> x0, waiting for transfers between devices: 77 us -> none  [the longest x1 77 us: on_device(): lax.psum_scatter(correction, 'view', scatter_dimension=1, tiled=True)]
    add x11 -> x7, other arithmetic: 34.4 us -> 0.13 us  [the longest x1 0.1 us: on_device(): table_xz = table_xz + share[:, :, None] * taken[:, side][:, None, :]]
    slice x10 -> x16, local copies, waits for them, and re-layouts: 20.6 us -> 10.6 us  [the longest x1 6.25 us: on_device(): piece = lax.dynamic_slice_in_dim(raw_tiles[slot], other_start, quo_rows, 1)]
    reduce_sum x7 -> x6, other arithmetic: 9.76 us -> 0.74 us  [the longest x4 0.49 us: inside_sum(): return jnp.sum(jnp.where(inside, kernel[:, None, :], 0.0), axis=2)]
  transfers between devices with their start and end apart: 9 -> 9, of which waited for: 4 -> 2; matrix products, arithmetic and copies ran while one was open for 55% -> 22% of each run, Pallas kernels for 0% -> 39%
where the time goes in v1:
time: 181 us; the launch traced here: 178 us
  Pallas kernels  92.9 us (51%)
  starting transfers between devices  22 us (12%)
  local copies, waits for them, and re-layouts  21.8 us (12%)
  other arithmetic  21.5 us (12%)
  waiting for transfers between devices  17.8 us (10%)
    pallas_call x4, Pallas kernels, view_pass(): pl.pallas_call(view_kernel, grid_spec=pltpu.PrefetchScalarGridSpec(num_sc...  69.2 us
    pallas_call x2, Pallas kernels, rows_forward(): pl.pallas_call(rows_forward_kernel, grid=(count // PLANES,), in_specs=[pl...  12.1 us
    pallas_call x2, Pallas kernels, rows_back(): pl.pallas_call(rows_back_kernel, grid=(blocks,), in_specs=[pl.BlockSpec((...  11.6 us
    ppermute x1, waiting for transfers between devices, on_device(): low = lax.ppermute(edges[halo:], 'tile', up)  9.23 us
    ppermute x1, waiting for transfers between devices, on_device(): lax.ppermute(inner_est[block - halo:], 'tile', up)  8.6 us
    slice x1, local copies, waits for them, and re-layouts, on_device(): piece = lax.dynamic_slice_in_dim(raw_tiles[slot], other_start, quo_rows, 1)  6.25 us
    ppermute x1, starting transfers between devices, on_device(): lax.ppermute(depth_range, 'tile', up)  4.5 us
    ppermute x1, starting transfers between devices, on_device(): lax.ppermute(inner_est[block - halo:], 'tile', up)  4.48 us
  transfers between devices with their start and end apart: 9, of which 2 were waited for; matrix products, arithmetic and copies ran while one was open for 22% of the time, Pallas kernels for 39%

profile of v1, /device:TPU:1, one launch (start us, length us, event | category | flops | bytes accessed | tf_op | source)
XLA Modules:
  0.0 177.7 jit_solution(7589933892670113667)
XLA Ops:
  0.0 4.5 %collective-permute-start.3 = (s32[4,1,2]{0,2,1:T(2,128)}, s32[4,1,2]{0,2,1:T(2,128)S(1)}, u32[]{:S(2)}, u32[]{:S(2)}) collective-permute-start(s32[4,1,2]{0,2,1:T(2,128)} %param.9), channel_id=1, source_target_pairs={{0,1},{1,2},{2,3},{3,4},{4,5},{5,6},{6,7},{7,8},{8,9},{9,10},{10,1... | collective-permute-start | bytes 104 | tf_op jit(solution)/shard_map/ppermute | solution.py:249
  4.5 1.9 %collective-permute-start.4 = (s32[4,1,2]{0,2,1:T(2,128)}, s32[4,1,2]{0,2,1:T(2,128)S(1)}, u32[]{:S(2)}, u32[]{:S(2)}) collective-permute-start(s32[4,1,2]{0,2,1:T(2,128)} %param.9), channel_id=1, source_target_pairs={{1,0},{2,1},{3,2},{4,3},{5,4},{6,5},{7,6},{8,7},{9,8},{10,9},{11,1... | collective-permute-start | bytes 104 | tf_op jit(solution)/shard_map/ppermute | solution.py:251
  6.4 2.2 %add_convert_fusion = bf16[24,256,128]{2,1,0:T(8,128)(2,1)S(1)} fusion(f32[24,256,128]{2,1,0:T(8,128)} %param.5), kind=kLoop, calls=%fused_computation.1 | loop fusion | flops 1572864 | bytes 4718592 | tf_op jit(solution)/shard_map/convert_element_type | solution.py:222
  9.5 1.2 collective-permute-start
  10.7 6.3 %fusion.221 = (bf16[1,24,512,128]{3,2,1,0:T(8,128)(2,1)}, bf16[1,24,512,128]{3,2,1,0:T(8,128)(2,1)}) fusion(bf16[2,24,512,128]{3,2,1,0:T(8,128)(2,1)} %raw_ref.3), kind=kLoop, calls=%fused_computation.364 | loop fusion | bytes 12582912 | tf_op jit(solution)/shard_map/slice | solution.py:236
  17.0 3.0 %dynamic-slice_bitcast_fusion = bf16[24,272,128]{2,1,0:T(8,128)(2,1)} fusion(bf16[1,24,512,128]{3,2,1,0:T(8,128)(2,1)} %get-tuple-element.82, s32[]{:T(128)S(6)} %select_n.937), kind=kLoop, calls=%fused_computation.6 | loop fusion | bytes 3342340 | tf_op jit(solution)/shard_map/dynamic_slice | solution.py:236
  20.2 1.3 dynamic-slice_bitcast_fusion.1
  21.5 1.2 collective-permute-start.5
  23.6 1.4 select_convert_fusion.1.plane_t_ref
  24.9 1.2 select_convert_fusion.3.plane_ref
  34.4 1.9 %select_convert_fusion.2.refs_4_ = bf16[256,1088]{1,0:T(8,128)(2,1)S(1)} fusion(bf16[1088]{0:T(1024)(128)(2,1)S(1)} %broadcast_in_dim.870, bf16[1088]{0:T(1024)(128)(2,1)S(1)} %broadcast_in_dim.866, bf16[1088]{0:T(1024)(128)(2,1)S(1)} %broadcast_in_dim.862, bf16[1088]{0:T(1024)(128)(2,1)S(1)} %broadcast_in_dim.858, ...), kind=kLoop, calls=%fused_computation.49 | loop fusion | flops 10305536 | bytes 603776 | tf_op jit(solution)/shard_map/convert_element_type | solution.py:291
  36.3 3.8 %select_convert_fusion.matrix_ref = bf16[1088,288]{1,0:T(8,128)(2,1)S(1)} fusion(bf16[1088]{0:T(1024)(128)(2,1)S(1)} %broadcast_in_dim.870, bf16[1088]{0:T(1024)(128)(2,1)S(1)} %broadcast_in_dim.866, bf16[1088]{0:T(1024)(128)(2,1)S(1)} %broadcast_in_dim.862, bf16[1088]{0:T(1024)(128)(2,1)S(1)} %broadcast_in_dim.858, ...), kind=kLoop, calls=%fused_computation.8 | loop fusion | flops 11907072 | bytes 674976 | tf_op jit(solution)/shard_map/convert_element_type | solution.py:285
  40.1 1.3 pad_add_fusion
  41.4 1.3 pad_add_fusion.2
  44.3 1.5 fusion.68
  45.8 4.5 %collective-permute-start.1 = (bf16[12,288,128]{2,1,0:T(8,128)(2,1)S(1)}, bf16[12,288,128]{2,1,0:T(8,128)(2,1)S(1)}, u32[]{:S(2)}, u32[]{:S(2)}) collective-permute-start(bf16[12,288,128]{2,1,0:T(8,128)(2,1)S(1)} %get-tuple-element.84), channel_id=1, source_target_pairs={{0,1},{1,2},{2,3},{3,4},{4,5},{5,6},{6,7},{7,8},{8,9},{9,10},{10,1... | collective-permute-start | bytes 2654216 | tf_op jit(solution)/shard_map/ppermute | solution.py:227
  50.3 2.1 %collective-permute-start.2 = (bf16[12,288,128]{2,1,0:T(8,128)(2,1)S(1)}, bf16[12,288,128]{2,1,0:T(8,128)(2,1)S(1)}, u32[]{:S(2)}, u32[]{:S(2)}) collective-permute-start(bf16[12,288,128]{2,1,0:T(8,128)(2,1)S(1)} %get-tuple-element.85), channel_id=1, source_target_pairs={{1,0},{2,1},{3,2},{4,3},{5,4},{6,5},{7,6},{8,7},{9,8},{10,9},{11,1... | collective-permute-start | bytes 2654216 | tf_op jit(solution)/shard_map/ppermute | solution.py:228
  54.1 1.0 pad_maximum_fusion.est_ref
  55.1 6.0 %shard_map.55.inner_ref = bf16[4,24,272,128]{3,2,1,0:T(8,128)(2,1)} custom-call(bf16[24,288,128]{2,1,0:T(8,128)(2,1)S(1)} %pad_maximum_fusion.est_ref, bf16[1088,288]{1,0:T(8,128)(2,1)S(1)} %select_convert_fusion.matrix_ref), custom_call_target="tpu_custom_call" | custom-call | flops 1925185536 | bytes 8454144 | tf_op jit(solution)/shard_map/pallas_call | solution.py:45
  61.2 8.6 %collective-permute-done.1 = bf16[12,288,128]{2,1,0:T(8,128)(2,1)S(1)} collective-permute-done((bf16[12,288,128]{2,1,0:T(8,128)(2,1)S(1)}, bf16[12,288,128]{2,1,0:T(8,128)(2,1)S(1)}, u32[]{:S(2)}, u32[]{:S(2)}) %collective-permute-start.1) | collective-permute-done | bytes 884768 | tf_op jit(solution)/shard_map/ppermute | solution.py:227
  69.9 6.1 %shard_map.56.outer_ref = bf16[4,24,272,128]{3,2,1,0:T(8,128)(2,1)} custom-call(bf16[24,288,128]{2,1,0:T(8,128)(2,1)S(1)} %pad_maximum_fusion.1.est_ref, bf16[1088,288]{1,0:T(8,128)(2,1)S(1)} %select_convert_fusion.matrix_ref), custom_call_target="tpu_custom_call" | custom-call | flops 1925185536 | bytes 8454144 | tf_op jit(solution)/shard_map/pallas_call | solution.py:45
  76.2 16.6 %shard_map.58.refs_1_ = bf16[48,272,128]{2,1,0:T(8,128)(2,1)S(1)} custom-call(s32[2]{0:T(128)S(1)} %get-tuple-element.128.scalar_ref, bf16[4,24,272,128]{3,2,1,0:T(8,128)(2,1)} %shard_map.55.inner_ref, bf16[4,24,272,128]{3,2,1,0:T(8,128)(2,1)} %shard_map.56.outer_ref, bf16[2,24,512,128]{3,2,1,0:T(8,128)(2,1)} %raw_ref.3, ...), custom_call_target="tpu_custom_call" | custom-call | flops 4456448000 | bytes 8355840 | tf_op jit(solution)/shard_map/pallas_call | solution.py:129
  92.9 1.7 copy-done
  94.6 16.6 %shard_map.57.refs_0_ = bf16[48,272,128]{2,1,0:T(8,128)(2,1)S(1)} custom-call(s32[2]{0:T(128)S(1)} %get-tuple-element.127.scalar_ref, bf16[4,24,272,128]{3,2,1,0:T(8,128)(2,1)} %shard_map.55.inner_ref, bf16[4,24,272,128]{3,2,1,0:T(8,128)(2,1)} %shard_map.56.outer_ref, bf16[2,24,512,128]{3,2,1,0:T(8,128)(2,1)} %raw_ref.3, ...), custom_call_target="tpu_custom_call" | custom-call | flops 4456448000 | bytes 8355840 | tf_op jit(solution)/shard_map/pallas_call | solution.py:129
  111.2 18.1 %shard_map.60.refs_3_ = bf16[48,272,128]{2,1,0:T(8,128)(2,1)} custom-call(s32[2]{0:T(128)S(1)} %get-tuple-element.125.scalar_ref, bf16[4,24,272,128]{3,2,1,0:T(8,128)(2,1)} %shard_map.55.inner_ref, bf16[4,24,272,128]{3,2,1,0:T(8,128)(2,1)} %shard_map.56.outer_ref, bf16[1,24,272,128]{3,2,1,0:T(8,128)(2,1)} %bitcast.19.raw_ref, ...), custom_call_target="tpu_custom_call" | custom-call | flops 4456448000 | bytes 8355840 | tf_op jit(solution)/shard_map/pallas_call | solution.py:129
  129.4 17.8 %shard_map.59.refs_2_ = bf16[48,272,128]{2,1,0:T(8,128)(2,1)} custom-call(s32[2]{0:T(128)S(1)} %get-tuple-element.126.scalar_ref, bf16[4,24,272,128]{3,2,1,0:T(8,128)(2,1)} %shard_map.55.inner_ref, bf16[4,24,272,128]{3,2,1,0:T(8,128)(2,1)} %shard_map.56.outer_ref, bf16[1,24,272,128]{3,2,1,0:T(8,128)(2,1)} %bitcast.17.raw_ref, ...), custom_call_target="tpu_custom_call" | custom-call | flops 4456448000 | bytes 8355840 | tf_op jit(solution)/shard_map/pallas_call | solution.py:129
  147.2 5.6 %shard_map.62 = bf16[24,256,128]{2,1,0:T(8,128)(2,1)S(1)} custom-call(bf16[48,272,128]{2,1,0:T(8,128)(2,1)S(1)} %shard_map.57.refs_0_, bf16[48,272,128]{2,1,0:T(8,128)(2,1)} %copy-done, bf16[48,272,128]{2,1,0:T(8,128)(2,1)} %shard_map.59.refs_2_, bf16[48,272,128]{2,1,0:T(8,128)(2,1)} %shard_map.60.refs_3_, bf16[256,1088]{1,0:T(8,128)(2,1)S(1)} %select_convert_fusion.2.refs_4_), custom_call_target="tpu_custom_call" | custom-call | flops 1711276032 | bytes 9830400 | tf_op jit(solution)/shard_map/pallas_call | solution.py:188
  152.9 4.4 %collective-permute-start.7 = (bf16[12,256,128]{2,1,0:T(8,128)(2,1)S(1)}, bf16[12,256,128]{2,1,0:T(8,128)(2,1)S(1)}, u32[]{:S(2)}, u32[]{:S(2)}) collective-permute-start(bf16[12,256,128]{2,1,0:T(8,128)(2,1)S(1)} %get-tuple-element.86), channel_id=1, source_target_pairs={{0,1},{1,2},{2,3},{3,4},{4,5},{5,6},{6,7},{7,8},{8,9},{9,10},{10,1... | collective-permute-start | bytes 2359304 | tf_op jit(solution)/shard_map/ppermute | solution.py:358
  157.3 1.9 %collective-permute-start.8 = (bf16[12,256,128]{2,1,0:T(8,128)(2,1)S(1)}, bf16[12,256,128]{2,1,0:T(8,128)(2,1)S(1)}, u32[]{:S(2)}, u32[]{:S(2)}) collective-permute-start(bf16[12,256,128]{2,1,0:T(8,128)(2,1)S(1)} %get-tuple-element.87), channel_id=1, source_target_pairs={{1,0},{2,1},{3,2},{4,3},{5,4},{6,5},{7,6},{8,7},{9,8},{10,9},{11,1... | collective-permute-start | bytes 2359304 | tf_op jit(solution)/shard_map/ppermute | solution.py:359
  159.4 6.0 %shard_map.61 = f32[24,256,128]{2,1,0:T(8,128)S(1)} custom-call(bf16[48,272,128]{2,1,0:T(8,128)(2,1)} %copy-done.1, bf16[48,272,128]{2,1,0:T(8,128)(2,1)} %copy-done, bf16[48,272,128]{2,1,0:T(8,128)(2,1)} %shard_map.59.refs_2_, bf16[48,272,128]{2,1,0:T(8,128)(2,1)} %shard_map.60.refs_3_, bf16[256,1088]{1,0:T(8,128)(2,1)S(1)} %select_convert_fusion.2.refs_4_), custom_call_target="tpu_custom_call" | custom-call | flops 1711276032 | bytes 9830400 | tf_op jit(solution)/shard_map/pallas_call | solution.py:188
  165.4 9.2 %collective-permute-done.7 = bf16[12,256,128]{2,1,0:T(8,128)(2,1)S(1)} collective-permute-done((bf16[12,256,128]{2,1,0:T(8,128)(2,1)S(1)}, bf16[12,256,128]{2,1,0:T(8,128)(2,1)S(1)}, u32[]{:S(2)}, u32[]{:S(2)}) %collective-permute-start.7) | collective-permute-done | bytes 786464 | tf_op jit(solution)/shard_map/ppermute | solution.py:358
  174.6 3.0 %maximum_divide_fusion = f32[24,256,128]{2,1,0:T(8,128)} fusion(f32[24,256,128]{2,1,0:T(8,128)S(1)} %copy-done.4, f32[24,256,128]{2,1,0:T(8,128)S(1)} %shard_map.61, f32[256]{0:T(256)S(1)} %bitcast.54, f32[24,128]{1,0:T(8,128)S(1)} %get-tuple-element.89, f32[256]{0:T(256)S(1)} %bitcast.55, f32[24,128]{1,0:T(8,128)S(1)} %get-tuple-element.90, ...), kind=kLoop, calls=%fused_computation | loop fusion | flops 12582912 | bytes 11063296 | tf_op jit(solution)/shard_map/div | solution.py:366
  (192 shorter events, 13.3 us)
Async XLA Ops:
  0.0 43.7 %collective-permute-start.3 = (s32[4,1,2]{0,2,1:T(2,128)}, s32[4,1,2]{0,2,1:T(2,128)S(1)}, u32[]{:S(2)}, u32[]{:S(2)}) collective-permute-start(s32[4,1,2]{0,2,1:T(2,128)} %param.9), channel_id=1, source_target_pairs={{0,1},{1,2},{2,3},{3,4},{4,5},{5,6},{6,7},{7,8},{8,9},{9,10},{10,1... | collective-permute-start | bytes 104 | tf_op jit(solution)/shard_map/ppermute | solution.py:249
  4.5 39.3 %collective-permute-start.4 = (s32[4,1,2]{0,2,1:T(2,128)}, s32[4,1,2]{0,2,1:T(2,128)S(1)}, u32[]{:S(2)}, u32[]{:S(2)}) collective-permute-start(s32[4,1,2]{0,2,1:T(2,128)} %param.9), channel_id=1, source_target_pairs={{1,0},{2,1},{3,2},{4,3},{5,4},{6,5},{7,6},{8,7},{9,8},{10,9},{11,1... | collective-permute-start | bytes 104 | tf_op jit(solution)/shard_map/ppermute | solution.py:251
  9.5 34.8 %collective-permute-start = (bf16[24,32,128]{2,1,0:T(8,128)(2,1)}, bf16[24,32,128]{2,1,0:T(8,128)(2,1)}, u32[]{:S(2)}, u32[]{:S(2)}) collective-permute-start(bf16[24,32,128]{2,1,0:T(8,128)(2,1)} %constant_dynamic-slice_fusion), channel_id=1, source_target_pairs={{0,16},{16,0},{1,17},{17,1},{2,18},{18,2},{3,19},{19,3},{4,20},{20... | collective-permute-start | bytes 589832 | tf_op jit(solution)/shard_map/ppermute | solution.py:224
  20.0 91.3 %collective-permute-start.6 = (bf16[24,272,128]{2,1,0:T(8,128)(2,1)}, bf16[24,272,128]{2,1,0:T(8,128)(2,1)}, u32[]{:S(2)}, u32[]{:S(2)}) collective-permute-start(bf16[24,272,128]{2,1,0:T(8,128)(2,1)} %dynamic-slice_bitcast_fusion), channel_id=1, source_target_pairs={{0,16},{16,0},{1,17},{17,1},{2,18},{18,2},{3,19},{19,3},{4,20},{20... | collective-permute-start | bytes 5013512 | tf_op jit(solution)/shard_map/ppermute | solution.py:237
  21.5 9.1 %copy-start.7 = (s32[4,3]{1,0:T(4,128)S(1)}, s32[4,3]{1,0:T(4,128)}, u32[]{:S(2)}) copy-start(s32[4,3]{1,0:T(4,128)} %param.8) | copy-start | bytes 148
  21.5 107.9 %collective-permute-start.5 = (bf16[24,272,128]{2,1,0:T(8,128)(2,1)}, bf16[24,272,128]{2,1,0:T(8,128)(2,1)}, u32[]{:S(2)}, u32[]{:S(2)}) collective-permute-start(bf16[24,272,128]{2,1,0:T(8,128)(2,1)} %dynamic-slice_bitcast_fusion.1), channel_id=1, source_target_pairs={{0,16},{16,0},{1,17},{17,1},{2,18},{18,2},{3,19},{19,3},{4,20},{20... | collective-permute-start | bytes 5013512 | tf_op jit(solution)/shard_map/ppermute | solution.py:237
  26.1 17.7 %copy-start.8 = (s32[4,1,2]{0,2,1:T(2,128)S(1)}, s32[4,1,2]{0,2,1:T(2,128)}, u32[]{:S(2)}) copy-start(s32[4,1,2]{0,2,1:T(2,128)} %param.9) | copy-start | bytes 100
  33.8 9.1 %copy-start.9 = (bf16[4]{0:T(256)(128)(2,1)S(1)}, bf16[4]{0:T(256)(128)(2,1)}, u32[]{:S(2)}) copy-start(bf16[4]{0:T(256)(128)(2,1)} %get-tuple-element.29) | copy-start | bytes 28
  33.8 9.1 %copy-start.10 = (bf16[4]{0:T(256)(128)(2,1)S(1)}, bf16[4]{0:T(256)(128)(2,1)}, u32[]{:S(2)}) copy-start(bf16[4]{0:T(256)(128)(2,1)} %get-tuple-element.30) | copy-start | bytes 28
  33.8 9.1 %copy-start.11 = (bf16[4]{0:T(256)(128)(2,1)S(1)}, bf16[4]{0:T(256)(128)(2,1)}, u32[]{:S(2)}) copy-start(bf16[4]{0:T(256)(128)(2,1)} %get-tuple-element.31) | copy-start | bytes 28
  33.8 9.1 %copy-start.12 = (bf16[4]{0:T(256)(128)(2,1)S(1)}, bf16[4]{0:T(256)(128)(2,1)}, u32[]{:S(2)}) copy-start(bf16[4]{0:T(256)(128)(2,1)} %get-tuple-element.32) | copy-start | bytes 28
  33.8 9.1 %copy-start.13 = (bf16[4]{0:T(256)(128)(2,1)S(1)}, bf16[4]{0:T(256)(128)(2,1)}, u32[]{:S(2)}) copy-start(bf16[4]{0:T(256)(128)(2,1)} %get-tuple-element.33) | copy-start | bytes 28
  33.8 9.1 %copy-start.14 = (bf16[4]{0:T(256)(128)(2,1)S(1)}, bf16[4]{0:T(256)(128)(2,1)}, u32[]{:S(2)}) copy-start(bf16[4]{0:T(256)(128)(2,1)} %get-tuple-element.34) | copy-start | bytes 28
  33.8 9.1 %copy-start.15 = (bf16[4]{0:T(256)(128)(2,1)S(1)}, bf16[4]{0:T(256)(128)(2,1)}, u32[]{:S(2)}) copy-start(bf16[4]{0:T(256)(128)(2,1)} %get-tuple-element.35) | copy-start | bytes 28
  33.8 9.1 %copy-start.16 = (bf16[4]{0:T(256)(128)(2,1)S(1)}, bf16[4]{0:T(256)(128)(2,1)}, u32[]{:S(2)}) copy-start(bf16[4]{0:T(256)(128)(2,1)} %get-tuple-element.36) | copy-start | bytes 28
  33.8 9.1 %copy-start.17 = (bf16[4]{0:T(256)(128)(2,1)S(1)}, bf16[4]{0:T(256)(128)(2,1)}, u32[]{:S(2)}) copy-start(bf16[4]{0:T(256)(128)(2,1)} %get-tuple-element.37) | copy-start | bytes 28
  33.8 9.1 %copy-start.18 = (bf16[4]{0:T(256)(128)(2,1)S(1)}, bf16[4]{0:T(256)(128)(2,1)}, u32[]{:S(2)}) copy-start(bf16[4]{0:T(256)(128)(2,1)} %get-tuple-element.38) | copy-start | bytes 28
  33.9 9.1 %copy-start.19 = (bf16[4]{0:T(256)(128)(2,1)S(1)}, bf16[4]{0:T(256)(128)(2,1)}, u32[]{:S(2)}) copy-start(bf16[4]{0:T(256)(128)(2,1)} %get-tuple-element.39) | copy-start | bytes 28
  33.9 9.1 %copy-start.20 = (bf16[4]{0:T(256)(128)(2,1)S(1)}, bf16[4]{0:T(256)(128)(2,1)}, u32[]{:S(2)}) copy-start(bf16[4]{0:T(256)(128)(2,1)} %get-tuple-element.40) | copy-start | bytes 28
  33.9 9.1 %copy-start.21 = (bf16[4]{0:T(256)(128)(2,1)S(1)}, bf16[4]{0:T(256)(128)(2,1)}, u32[]{:S(2)}) copy-start(bf16[4]{0:T(256)(128)(2,1)} %get-tuple-element.41) | copy-start | bytes 28
  33.9 9.1 %copy-start.22 = (bf16[4]{0:T(256)(128)(2,1)S(1)}, bf16[4]{0:T(256)(128)(2,1)}, u32[]{:S(2)}) copy-start(bf16[4]{0:T(256)(128)(2,1)} %get-tuple-element.42) | copy-start | bytes 28
  33.9 9.1 %copy-start.23 = (bf16[4]{0:T(256)(128)(2,1)S(1)}, bf16[4]{0:T(256)(128)(2,1)}, u32[]{:S(2)}) copy-start(bf16[4]{0:T(256)(128)(2,1)} %get-tuple-element.43) | copy-start | bytes 28
  33.9 9.1 %copy-start.24 = (bf16[4]{0:T(256)(128)(2,1)S(1)}, bf16[4]{0:T(256)(128)(2,1)}, u32[]{:S(2)}) copy-start(bf16[4]{0:T(256)(128)(2,1)} %get-tuple-element.44) | copy-start | bytes 28
  33.9 9.1 %copy-start.25 = (bf16[4]{0:T(256)(128)(2,1)S(1)}, bf16[4]{0:T(256)(128)(2,1)}, u32[]{:S(2)}) copy-start(bf16[4]{0:T(256)(128)(2,1)} %get-tuple-element.45) | copy-start | bytes 28
  44.1 8.4 %copy-start.30 = (f32[4]{0:T(128)S(1)}, f32[4]{0:T(128)}, u32[]{:S(2)}) copy-start(f32[4]{0:T(128)} %get-tuple-element.13) | copy-start | bytes 52
  44.2 8.4 %copy-start.31 = (f32[4]{0:T(128)S(1)}, f32[4]{0:T(128)}, u32[]{:S(2)}) copy-start(f32[4]{0:T(128)} %get-tuple-element.14) | copy-start | bytes 52
  45.8 23.9 %collective-permute-start.1 = (bf16[12,288,128]{2,1,0:T(8,128)(2,1)S(1)}, bf16[12,288,128]{2,1,0:T(8,128)(2,1)S(1)}, u32[]{:S(2)}, u32[]{:S(2)}) collective-permute-start(bf16[12,288,128]{2,1,0:T(8,128)(2,1)S(1)} %get-tuple-element.84), channel_id=1, source_target_pairs={{0,1},{1,2},{2,3},{3,4},{4,5},{5,6},{6,7},{7,8},{8,9},{9,10},{10,1... | collective-permute-start | bytes 2654216 | tf_op jit(solution)/shard_map/ppermute | solution.py:227
  50.3 19.4 %collective-permute-start.2 = (bf16[12,288,128]{2,1,0:T(8,128)(2,1)S(1)}, bf16[12,288,128]{2,1,0:T(8,128)(2,1)S(1)}, u32[]{:S(2)}, u32[]{:S(2)}) collective-permute-start(bf16[12,288,128]{2,1,0:T(8,128)(2,1)S(1)} %get-tuple-element.85), channel_id=1, source_target_pairs={{1,0},{2,1},{3,2},{4,3},{5,4},{6,5},{7,6},{8,7},{9,8},{10,9},{11,1... | collective-permute-start | bytes 2654216 | tf_op jit(solution)/shard_map/ppermute | solution.py:228
  111.2 36.0 %copy-start.1 = (bf16[48,272,128]{2,1,0:T(8,128)(2,1)}, bf16[48,272,128]{2,1,0:T(8,128)(2,1)S(1)}, u32[]{:S(2)}) copy-start(bf16[48,272,128]{2,1,0:T(8,128)(2,1)S(1)} %shard_map.57.refs_0_) | copy-start | bytes 10027012
  152.9 21.7 %collective-permute-start.7 = (bf16[12,256,128]{2,1,0:T(8,128)(2,1)S(1)}, bf16[12,256,128]{2,1,0:T(8,128)(2,1)S(1)}, u32[]{:S(2)}, u32[]{:S(2)}) collective-permute-start(bf16[12,256,128]{2,1,0:T(8,128)(2,1)S(1)} %get-tuple-element.86), channel_id=1, source_target_pairs={{0,1},{1,2},{2,3},{3,4},{4,5},{5,6},{6,7},{7,8},{8,9},{9,10},{10,1... | collective-permute-start | bytes 2359304 | tf_op jit(solution)/shard_map/ppermute | solution.py:358
  157.3 17.3 %collective-permute-start.8 = (bf16[12,256,128]{2,1,0:T(8,128)(2,1)S(1)}, bf16[12,256,128]{2,1,0:T(8,128)(2,1)S(1)}, u32[]{:S(2)}, u32[]{:S(2)}) collective-permute-start(bf16[12,256,128]{2,1,0:T(8,128)(2,1)S(1)} %get-tuple-element.87), channel_id=1, source_target_pairs={{1,0},{2,1},{3,2},{4,3},{5,4},{6,5},{7,6},{8,7},{9,8},{10,9},{11,1... | collective-permute-start | bytes 2359304 | tf_op jit(solution)/shard_map/ppermute | solution.py:359
  159.4 15.3 %copy-start.4 = (f32[24,256,128]{2,1,0:T(8,128)S(1)}, f32[24,256,128]{2,1,0:T(8,128)}, u32[]{:S(2)}) copy-start(f32[24,256,128]{2,1,0:T(8,128)} %param.5) | copy-start | bytes 9437188
  (21 other events, 149.3 us)

commit v2 on v1

v2 whole, which is shorter than its diff:
```python
import functools

import jax
import jax.numpy as jnp
from jax import lax
from jax.experimental import pallas as pl
from jax.experimental.pallas import tpu as pltpu
from jax.sharding import PartitionSpec as P

MAXOFF = 4
BACKGROUND = 0.1
FLOOR = 0.5
EST_MID = 1.25
QUO_MID = 1.1875
SUB = 8
ROWS = 16
PLANES = 4
F32 = jnp.float32
BF16 = jnp.bfloat16
VMEM_LIMIT = 48 * 1024 * 1024


def banded(taps, number):
    total = jnp.zeros(number.shape, F32)
    for index, tap in enumerate(taps):
        total = jnp.where(number == index, tap, total)
    return total


def inside_sum(taps, first, step, low, high):
    total = jnp.zeros(first.shape, F32)
    for index, tap in enumerate(taps):
        at = first + step * index
        total = total + jnp.where((at >= low) & (at < high), tap, 0.0)
    return total


def tables_kernel(
    exact_ref,
    rounded_ref,
    scale_in_ref,
    offset_ref,
    range_ref,
    position_ref,
    rows_ref,
    rows_t_ref,
    plane_ref,
    plane_t_ref,
    depth_ref,
    depth_t_ref,
    ones_x_ref,
    ones_yz_ref,
    cover_ref,
    scale_ref,
    *,
    slots,
    tiles,
    rows_all,
):
    views, _, taps = exact_ref.shape
    half = taps // 2
    half_rows = rows_t_ref.shape[0]
    quo_rows = ones_yz_ref.shape[1]
    est_rows = rows_ref.shape[1]
    est_extra = est_rows - half_rows
    block, depth = ones_x_ref.shape[1], ones_x_ref.shape[3]
    place, tile = position_ref[0], position_ref[1]
    quo_first = place * (half_rows - ROWS)
    order = [lax.rem(place * slots + w, views) for w in range(views)]
    rounded = [
        [[rounded_ref[w, d, a] for a in range(taps)] for d in range(3)] for w in order
    ]
    exact = [[[exact_ref[w, d, a] for a in range(taps)] for d in range(3)] for w in order]
    offsets = [[offset_ref[w, d] for d in range(3)] for w in order]

    def iota(shape, dim):
        return lax.broadcasted_iota(jnp.int32, shape, dim)

    for w in range(views):
        ox, oy, oz = offsets[w]

        def plane_rows(i, carry, w=w):
            shape = (ROWS, plane_ref.shape[2])
            row, column = iota(shape, 0) + i * ROWS, iota(shape, 1)
            step = jnp.where(
                (row & (SUB - 1)) == (column & (SUB - 1)), (column >> 3) - (row >> 3), -1
            )
            at = pl.ds(pl.multiple_of(i * ROWS, ROWS), ROWS)
            plane_ref[w, at] = banded(rounded[w][0], step).astype(BF16)
            return carry

        lax.fori_loop(0, plane_ref.shape[1] // ROWS, plane_rows, 0)

        def plane_t_rows(i, carry, w=w):
            shape = (ROWS, plane_t_ref.shape[2])
            row, column = iota(shape, 0) + i * ROWS, iota(shape, 1)
            step = jnp.where(
                (row & (SUB - 1)) == (column & (SUB - 1)), (row >> 3) - (column >> 3), -1
            )
            at = pl.ds(pl.multiple_of(i * ROWS, ROWS), ROWS)
            plane_t_ref[w, at] = banded(rounded[w][0], step).astype(BF16)
            return carry

        lax.fori_loop(0, plane_t_ref.shape[1] // ROWS, plane_t_rows, 0)

        def depth_rows(i, carry, w=w, oz=oz):
            shape = (ROWS, depth)
            away = iota(shape, 0) + i * ROWS - iota(shape, 1)
            at = pl.ds(pl.multiple_of(i * ROWS, ROWS), ROWS)
            depth_ref[w, at] = banded(rounded[w][2], away - oz + half).astype(BF16)
            depth_t_ref[w, at] = banded(rounded[w][2], half - oz - away).astype(BF16)
            return carry

        lax.fori_loop(0, depth // ROWS, depth_rows, 0)

        def forward_rows(i, carry, w=w, oy=oy):
            shape = (ROWS, est_rows)
            position = iota(shape, 1)
            from_row = jnp.where(
                position < half_rows,
                place * half_rows + position,
                (1 - place) * half_rows
                + place * (half_rows - est_extra)
                + position
                - half_rows,
            )
            to_row = quo_first + i * ROWS + iota(shape, 0)
            value = banded(rounded[w][1], from_row - to_row - oy + half).astype(BF16)
            at = pl.multiple_of(w * quo_rows + i * ROWS, ROWS)
            rows_ref[pl.ds(at, ROWS)] = value
            return carry

        lax.fori_loop(0, quo_rows // ROWS, forward_rows, 0)

        shape = (block, SUB, depth)
        first = tile * block + iota(shape, 0) + ox - half
        ones_x_ref[w] = inside_sum(exact[w][0], first, 1, 0, tiles * block)
        first = quo_first + iota((quo_rows, depth), 0) + oy - half
        ones_y = inside_sum(exact[w][1], first, 1, 0, rows_all)
        shape = (SUB, depth)
        z = iota(shape, 1)
        ones_z = inside_sum(exact[w][2], z + oz - half, 1, 0, depth)
        ones_yz_ref[w] = EST_MID * ones_y * ones_z[:1]
        low, high = range_ref[order[w], 0, 0], range_ref[order[w], 0, 1]
        cover_ref[w] = jnp.where((z >= low) & (z < high), 1.0, 0.0)
        scale_ref[w] = jnp.full(shape, scale_in_ref[order[w]], F32)

    def back_rows(i, carry):
        shape = (ROWS, quo_rows)
        away = place * half_rows + i * ROWS + iota(shape, 0) - quo_first - iota(shape, 1)
        value = [banded(rounded[w][1], away - offsets[w][1] + half) for w in range(views)]
        at = pl.ds(pl.multiple_of(i * ROWS, ROWS), ROWS)
        rows_t_ref[at] = jnp.concatenate(value, axis=1).astype(BF16)
        return carry

    lax.fori_loop(0, half_rows // ROWS, back_rows, 0)


def weight_tables_kernel(
    exact_ref, offset_ref, below_ref, range_ref, above_ref, position_ref, xz_ref, y_ref, *, rows_all
):
    views, _, taps = exact_ref.shape
    half = taps // 2
    block, depth = xz_ref.shape[1:]
    half_rows = y_ref.shape[1]
    place = position_ref[0]

    def iota(shape, dim):
        return lax.broadcasted_iota(jnp.int32, shape, dim)

    for w in range(views):
        ox, oy, oz = (offset_ref[w, d] for d in range(3))
        exact = [[exact_ref[w, d, a] for a in range(taps)] for d in range(3)]
        plane = iota((block, depth), 0) - ox + half
        z = iota((SUB, depth), 1) - oz + half
        total = jnp.zeros((block, depth), F32)
        for side, limit in enumerate((below_ref, range_ref, above_ref)):
            low = (side - 1) * block
            share = inside_sum(exact[0], plane, -1, low, low + block)
            taken = inside_sum(exact[2], z, -1, limit[w, 0, 0], limit[w, 0, 1])
            total = total + share * taken[:1]
        xz_ref[w] = total
        first = place * half_rows + iota((half_rows, depth), 0) - oy + half
        y_ref[w] = inside_sum(exact[1], first, -1, 0, rows_all)


def finish_kernel(est_ref, kept_ref, low_ref, high_ref, xz_ref, y_ref, out_ref, *, sides):
    planes = est_ref.shape[0]
    views = y_ref.shape[0]
    step = pl.program_id(0)
    is_low = jnp.where(step < sides, 1.0, 0.0)
    for plane in range(planes):
        at = pl.ds(step * planes + plane, 1)
        weight = sum(y_ref[w] * xz_ref[w, at] for w in range(views))
        edge = low_ref[plane].astype(F32) * is_low + high_ref[plane].astype(F32) * (1.0 - is_low)
        correction = kept_ref[plane] + edge + QUO_MID * weight
        out_ref[plane] = est_ref[plane] * correction / jnp.maximum(weight, FLOOR)


def rows_forward_kernel(est_ref, matrix_ref, out_ref):
    views, groups, planes, _, depth = out_ref.shape
    rows = groups * ROWS
    for pair in range(0, planes, 2):
        data = jnp.concatenate([est_ref[pair], est_ref[pair + 1]], axis=1)
        done = jnp.dot(matrix_ref[...], data, preferred_element_type=F32).astype(BF16)
        for view in range(views):
            part = done[view * rows : (view + 1) * rows]
            out_ref[view, :, pair] = part[:, :depth].reshape(groups, ROWS, depth)
            out_ref[view, :, pair + 1] = part[:, depth:].reshape(groups, ROWS, depth)


def rows_forward(est, matrix, views):
    count, rows_in, depth = est.shape
    rows = matrix.shape[0] // views
    groups = rows // ROWS
    return pl.pallas_call(
        rows_forward_kernel,
        grid=(count // PLANES,),
        in_specs=[
            pl.BlockSpec((PLANES, rows_in, depth), lambda i: (i, 0, 0)),
            pl.BlockSpec(matrix.shape, lambda i: (0, 0)),
        ],
        out_specs=pl.BlockSpec(
            (views, groups, PLANES, ROWS, depth), lambda i: (0, 0, i, 0, 0)
        ),
        out_shape=jax.ShapeDtypeStruct((views, groups, count, ROWS, depth), BF16),
        compiler_params=pltpu.CompilerParams(vmem_limit_bytes=VMEM_LIMIT),
        cost_estimate=pl.CostEstimate(
            flops=2 * count * depth * rows_in * views * rows,
            bytes_accessed=2 * (est.size + views * count * rows * depth),
            transcendentals=0,
        ),
    )(est, matrix)


def view_kernel(
    scalar_ref,
    inner_ref,
    outer_ref,
    raw_ref,
    plane_ref,
    plane_t_ref,
    depth_ref,
    depth_t_ref,
    ones_x_ref,
    ones_yz_ref,
    cover_ref,
    scale_ref,
    out_ref,
    ext_ref,
):
    slots, block, _, depth = raw_ref.shape
    halo = outer_ref.shape[1] // 2
    window = plane_ref.shape[2] // SUB
    size = block * SUB
    every = range(slots)
    starts = [scalar_ref[1 + w] for w in every]
    ext_ref[:, :halo] = outer_ref[:, :halo]
    ext_ref[:, halo : halo + block] = inner_ref[...]
    ext_ref[:, halo + block :] = outer_ref[:, halo:]
    stacked = []
    for w in every:
        source = ext_ref[w, pl.ds(starts[w], window)].astype(F32)
        halves = [
            source[:, lo : lo + SUB].reshape(window * SUB, depth) for lo in range(0, ROWS, SUB)
        ]
        data = jnp.concatenate(halves, axis=1).astype(BF16)
        planes = jnp.dot(plane_ref[w], data, preferred_element_type=F32)
        stacked.append(
            jnp.concatenate([planes[:, :depth], planes[:, depth:]], axis=0).astype(BF16)
        )
    blurred = [
        jnp.dot(stacked[w], depth_ref[w], preferred_element_type=F32).reshape(
            2, block, SUB, depth
        )
        for w in every
    ]
    quotient = []
    for w in every:
        raw = raw_ref[w].astype(F32)
        scale = scale_ref[w]
        cover = cover_ref[w] * scale
        halves = []
        for half in range(2):
            ones_yz = ones_yz_ref[w, half * SUB : (half + 1) * SUB]
            predicted = blurred[w][half] * scale + ones_x_ref[w] * ones_yz
            ratio = raw[:, half * SUB : (half + 1) * SUB] / (predicted + BACKGROUND)
            halves.append((cover * (ratio - QUO_MID)).reshape(size, depth))
        quotient.append(jnp.concatenate(halves, axis=0).astype(BF16))
    back = [
        jnp.dot(quotient[w], depth_t_ref[w], preferred_element_type=F32) for w in every
    ]
    out_ref[...] = jnp.zeros_like(out_ref)
    for w in every:
        wide = jnp.concatenate([back[w][:size], back[w][size:]], axis=1).astype(BF16)
        spread = jnp.dot(plane_t_ref[w], wide, preferred_element_type=F32)
        spread = [
            spread[:, lo : lo + depth].reshape(window, SUB, depth) for lo in (0, depth)
        ]
        out_ref[w, pl.ds(starts[w], window)] = jnp.concatenate(spread, axis=1).astype(
            out_ref.dtype
        )


def view_pass(pair, slots, first, groups, base, starts, inner, outer, raw, tables):
    _, _, block, _, depth = inner.shape
    halo2 = outer.shape[2]
    plane, plane_t, depth_m, depth_mt, ones_x, ones_yz, cover, scale = tables
    scalars = jnp.concatenate([base[None], starts]).astype(jnp.int32)

    def table(array):
        zeros = (0,) * (array.ndim - 1)
        return pl.BlockSpec((slots,) + array.shape[1:], lambda g, s: (pair,) + zeros)

    def grouped(planes):
        return pl.BlockSpec(
            (slots, None, planes, ROWS, depth), lambda g, s: (pair, first + g, 0, 0, 0)
        )

    return pl.pallas_call(
        view_kernel,
        grid_spec=pltpu.PrefetchScalarGridSpec(
            num_scalar_prefetch=1,
            grid=(groups,),
            in_specs=[
                grouped(block),
                grouped(halo2),
                pl.BlockSpec((slots, block, ROWS, depth), lambda g, s: (0, 0, s[0] + g, 0)),
                table(plane),
                table(plane_t),
                table(depth_m),
                table(depth_mt),
                table(ones_x),
                pl.BlockSpec((slots, ROWS, depth), lambda g, s: (pair, first + g, 0)),
                table(cover),
                table(scale),
            ],
            out_specs=pl.BlockSpec(
                (slots, None, block + halo2, ROWS, depth), lambda g, s: (0, g, 0, 0, 0)
            ),
            scratch_shapes=[pltpu.VMEM((slots, block + halo2, ROWS, depth), BF16)],
        ),
        out_shape=jax.ShapeDtypeStruct((slots, groups, block + halo2, ROWS, depth), BF16),
        compiler_params=pltpu.CompilerParams(vmem_limit_bytes=VMEM_LIMIT),
        cost_estimate=pl.CostEstimate(
            flops=2 * slots * groups * 3_000 * 256 * 256,
            bytes_accessed=2 * slots * groups * ROWS * depth * (5 * block),
            transcendentals=slots * block * groups * ROWS * depth,
        ),
    )(scalars, inner, outer, raw, plane, plane_t, depth_m, depth_mt, ones_x, ones_yz, cover, scale)


def rows_back_kernel(*refs):
    *part_refs, matrix_ref, out_ref = refs
    own_ref, *other_refs = part_refs
    planes, _, depth = out_ref.shape

    def rows_of(ref, slot, plane):
        return ref[slot, :, plane].reshape(ref.shape[1] * ROWS, depth)

    for pair in range(0, planes, 2):
        pieces = []
        for refs_of in ((own_ref,), other_refs):
            for slot in range(own_ref.shape[0]):
                for ref in refs_of:
                    pieces.append(
                        jnp.concatenate(
                            [rows_of(ref, slot, pair), rows_of(ref, slot, pair + 1)], axis=1
                        )
                    )
        data = jnp.concatenate(pieces, axis=0)
        done = jnp.dot(matrix_ref[...], data, preferred_element_type=F32).astype(out_ref.dtype)
        out_ref[pair] = done[:, :depth]
        out_ref[pair + 1] = done[:, depth:]


def rows_back(parts, matrix, blocks, place, dtype):
    depth = parts[0].shape[-1]
    rows_out = matrix.shape[0]

    def planes_of(part):
        return pl.BlockSpec(
            part.shape[:2] + (PLANES, ROWS, depth), lambda i: (0, 0, place(i), 0, 0)
        )

    return pl.pallas_call(
        rows_back_kernel,
        grid=(blocks,),
        in_specs=[planes_of(part) for part in parts]
        + [pl.BlockSpec(matrix.shape, lambda i: (0, 0))],
        out_specs=pl.BlockSpec((PLANES, rows_out, depth), lambda i: (i, 0, 0)),
        out_shape=jax.ShapeDtypeStruct((blocks * PLANES, rows_out, depth), dtype),
        compiler_params=pltpu.CompilerParams(vmem_limit_bytes=VMEM_LIMIT),
        cost_estimate=pl.CostEstimate(
            flops=2 * blocks * PLANES * depth * matrix.size,
            bytes_accessed=2 * blocks * PLANES * depth * (matrix.shape[1] + 2 * rows_out),
            transcendentals=0,
        ),
    )(*parts, matrix)


def on_device(estimate, raw_tiles, psf_taps, view_offsets, depth_range):
    block, half_rows, depth = estimate.shape
    slots = raw_tiles.shape[0]
    views, _, taps = psf_taps.shape
    half = taps // 2
    halo = half + MAXOFF
    tiles = lax.axis_size("tile")
    place = lax.axis_index("view")
    rows_all = half_rows * lax.axis_size("view")
    swap = [(0, 1), (1, 0)]
    up = [(i, i + 1) for i in range(tiles - 1)]
    down = [(i + 1, i) for i in range(tiles - 1)]
    quo_rows = half_rows + ROWS
    groups = quo_rows // ROWS
    est_extra = 2 * ROWS
    window = block + taps - 1

    start = (1 - place) * (half_rows - est_extra)
    edge = lax.dynamic_slice_in_dim(estimate, start, est_extra, 1)
    edge = (edge - EST_MID).astype(BF16)
    centred = (estimate - EST_MID).astype(BF16)
    inner_est = jnp.concatenate([centred, lax.ppermute(edge, "view", swap)], axis=1)
    outer_est = jnp.concatenate(
        [
            lax.ppermute(inner_est[block - halo :], "tile", up),
            lax.ppermute(inner_est[:halo], "tile", down),
        ],
        axis=0,
    )

    other_start = (1 - place) * (half_rows - ROWS)
    cuts = [0, (groups + 1) // 2, groups]
    arrived = []
    for low, high in zip(cuts, cuts[1:]):
        piece = lax.dynamic_slice_in_dim(
            raw_tiles, other_start + low * ROWS, (high - low) * ROWS, 2
        )
        arrived.append(lax.ppermute(piece, "view", swap))

    kernels = psf_taps / jnp.sum(psf_taps, axis=2, keepdims=True)
    rounded = lax.reduce_precision(kernels, 8, 7)
    scale = 1.0 / jnp.prod(jnp.sum(rounded, axis=2), axis=1)
    position = jnp.stack([place, lax.axis_index("tile")]).astype(jnp.int32)

    smem = pl.BlockSpec(memory_space=pltpu.SMEM)
    vmem = pl.BlockSpec(memory_space=pltpu.VMEM)
    shapes = [
        ((views * quo_rows, half_rows + est_extra), BF16),
        ((half_rows, views * quo_rows), BF16),
        ((views, block * SUB, window * SUB), BF16),
        ((views, window * SUB, block * SUB), BF16),
        ((views, depth, depth), BF16),
        ((views, depth, depth), BF16),
        ((views, block, SUB, depth), F32),
        ((views, quo_rows, depth), F32),
        ((views, SUB, depth), F32),
        ((views, SUB, depth), F32),
    ]
    rows_m, rows_mt, *tables = pl.pallas_call(
        functools.partial(tables_kernel, slots=slots, tiles=tiles, rows_all=rows_all),
        in_specs=[smem] * 6,
        out_specs=[vmem] * len(shapes),
        out_shape=[jax.ShapeDtypeStruct(*shape) for shape in shapes],
        compiler_params=pltpu.CompilerParams(vmem_limit_bytes=VMEM_LIMIT),
        cost_estimate=pl.CostEstimate(flops=0, bytes_accessed=30_000_000, transcendentals=0),
    )(kernels, rounded, scale, view_offsets, depth_range, position)

    below = lax.ppermute(depth_range, "tile", up)
    above = lax.ppermute(depth_range, "tile", down)
    table_xz, table_y = pl.pallas_call(
        functools.partial(weight_tables_kernel, rows_all=rows_all),
        in_specs=[smem] * 6,
        out_specs=[vmem] * 2,
        out_shape=[
            jax.ShapeDtypeStruct((views, block, depth), F32),
            jax.ShapeDtypeStruct((views, half_rows, depth), F32),
        ],
        compiler_params=pltpu.CompilerParams(vmem_limit_bytes=VMEM_LIMIT),
        cost_estimate=pl.CostEstimate(flops=0, bytes_accessed=8_000_000, transcendentals=0),
    )(kernels, view_offsets, below, depth_range, above, position)

    inner = rows_forward(inner_est, rows_m, views)
    outer = rows_forward(outer_est, rows_m, views)
    own_first = lax.rem(place * slots + jnp.arange(views), views)
    starts = view_offsets[own_first, 0] + (halo - half)
    base = place * ((half_rows - ROWS) // ROWS)
    zero = jnp.zeros((), jnp.int32)
    parts = [
        view_pass(0, slots, 0, groups, base, starts[:slots], inner, outer, raw_tiles, tables)
    ]
    for low, high, piece in zip(cuts, cuts[1:], arrived):
        parts.append(
            view_pass(
                1, slots, low, high - low, zero, starts[slots:], inner, outer, piece, tables
            )
        )

    side = halo // PLANES
    middle = block // PLANES
    edges = rows_back(
        parts, rows_mt, 2 * side, lambda i: jnp.where(i < side, i, i + middle), BF16
    )
    kept = rows_back(parts, rows_mt, middle, lambda i: i + side, F32)
    low = lax.ppermute(edges[halo:], "tile", up)
    high = lax.ppermute(edges[:halo], "tile", down)
    sides = halo // PLANES
    whole = (PLANES, half_rows, depth)
    return pl.pallas_call(
        functools.partial(finish_kernel, sides=sides),
        grid=(middle,),
        in_specs=[
            pl.BlockSpec(whole, lambda i: (i, 0, 0)),
            pl.BlockSpec(whole, lambda i: (i, 0, 0)),
            pl.BlockSpec(whole, lambda i: (jnp.minimum(i, sides - 1), 0, 0)),
            pl.BlockSpec(whole, lambda i: (jnp.maximum(i - sides, 0), 0, 0)),
            pl.BlockSpec(table_xz.shape, lambda i: (0, 0, 0)),
            pl.BlockSpec(table_y.shape, lambda i: (0, 0, 0)),
        ],
        out_specs=pl.BlockSpec(whole, lambda i: (i, 0, 0)),
        out_shape=jax.ShapeDtypeStruct(estimate.shape, F32),
        compiler_params=pltpu.CompilerParams(vmem_limit_bytes=VMEM_LIMIT),
    )(estimate, kept, low, high, table_xz, table_y)


def solution(mesh):
    return jax.shard_map(
        on_device,
        mesh=mesh,
        in_specs=(
            P("tile", "view", None),
            P("view", "tile", None, None),
            P(),
            P(),
            P(None, "tile", None),
        ),
        out_specs=P("tile", "view", None),
        check_vma=False,
    )
```

time: 181 us -> 147 us (0.81)
  other arithmetic: 21.5 us -> 3.04 us
  local copies, waits for them, and re-layouts: 21.8 us -> 8.41 us
  waiting for transfers between devices: 17.8 us -> 20.7 us
    pallas_call x4 -> x3, Pallas kernels: 69.2 us -> 42.8 us  [view_pass(): pl.pallas_call(view_kernel, grid_spec=pltpu.PrefetchScalarGridSpec(num_sc...]
    pallas_call x2 -> x5, Pallas kernels: 11.6 us -> 35.9 us  [the longest x1 15.2 us: on_device(): pl.pallas_call(functools.partial(tables_kernel, slots=slots, tiles=tiles,...]
    slice x16 -> x2, local copies, waits for them, and re-layouts: 10.6 us -> 0.18 us  [the longest x1 0.1 us: on_device(): high = lax.ppermute(edges[:halo], 'tile', down)]
    ppermute x4, waiting for transfers between devices: 0.01 us -> 9.7 us  [the longest x1 9.7 us: on_device(): below = lax.ppermute(depth_range, 'tile', up)]
    ppermute x1, waiting for transfers between devices: 9.23 us -> 0.01 us  [on_device(): low = lax.ppermute(edges[halo:], 'tile', up)]
    convert_element_type x6 -> x1, other arithmetic: 8.94 us -> 1.72 us  [on_device(): edge = (edge - EST_MID).astype(BF16)]
    broadcast_in_dim x41 -> x0, local copies, waits for them, and re-layouts: 3.34 us -> none  [the longest x34 2.81 us: tap_lookup(): total = jnp.where(number == tap, value, total)]
    div x3 -> x0, other arithmetic: 3.05 us -> none  [the longest x1 3.04 us: on_device(): return estimate * correction / jnp.maximum(weight, FLOOR)]
  transfers between devices with their start and end apart: 9 -> 9, of which waited for: 2 -> 2; matrix products, arithmetic and copies ran while one was open for 22% -> 5% of each run, Pallas kernels for 39% -> 46%
where the time goes in v2:
time: 147 us; the launch traced here: 145 us
  Pallas kernels  91.1 us (62%)
  starting transfers between devices  22 us (15%)
  waiting for transfers between devices  20.7 us (14%)
  local copies, waits for them, and re-layouts  8.41 us (6%)
  other arithmetic  3.04 us (2%)
    pallas_call x3, Pallas kernels, view_pass(): pl.pallas_call(view_kernel, grid_spec=pltpu.PrefetchScalarGridSpec(num_sc...  42.8 us
    pallas_call x1, Pallas kernels, on_device(): pl.pallas_call(functools.partial(tables_kernel, slots=slots, tiles=tiles,...  15.2 us
    pallas_call x2, Pallas kernels, rows_forward(): pl.pallas_call(rows_forward_kernel, grid=(count // PLANES,), in_specs=[pl...  12.4 us
    pallas_call x2, Pallas kernels, rows_back(): pl.pallas_call(rows_back_kernel, grid=(blocks,), in_specs=[planes_of(part...  11.5 us
    ppermute x1, waiting for transfers between devices, on_device(): lax.ppermute(inner_est[block - halo:], 'tile', up)  11 us
    ppermute x1, waiting for transfers between devices, on_device(): below = lax.ppermute(depth_range, 'tile', up)  9.7 us
    pallas_call x1, Pallas kernels, on_device(): pl.pallas_call(functools.partial(finish_kernel, sides=sides), grid=(middl...  5.99 us
    dynamic_slice x2, local copies, waits for them, and re-layouts, on_device(): lax.dynamic_slice_in_dim(raw_tiles, other_start + low * ROWS, (high - low...  5.75 us
  transfers between devices with their start and end apart: 9, of which 2 were waited for; matrix products, arithmetic and copies ran while one was open for 5% of the time, Pallas kernels for 46%

profile of v2, /device:TPU:1, one launch (start us, length us, event | category | flops | bytes accessed | tf_op | source)
XLA Modules:
  0.0 145.4 jit_solution(6128194561395451476)
XLA Ops:
  0.0 1.7 %add_convert_fusion.1 = bf16[24,32,128]{2,1,0:T(8,128)(2,1)} fusion(f32[24,256,128]{2,1,0:T(8,128)} %est_ref.1, s32[]{:T(128)S(6)} %select_n.20), kind=kLoop, calls=%fused_computation.10 | loop fusion | flops 196608 | bytes 589828 | tf_op jit(solution)/shard_map/convert_element_type | solution.py:421
  1.7 2.1 %collective-permute-start = (bf16[24,32,128]{2,1,0:T(8,128)(2,1)}, bf16[24,32,128]{2,1,0:T(8,128)(2,1)S(1)}, u32[]{:S(2)}, u32[]{:S(2)}) collective-permute-start(bf16[24,32,128]{2,1,0:T(8,128)(2,1)} %add_convert_fusion.1), channel_id=1, source_target_pairs={{0,16},{16,0},{1,17},{17,1},{2,18},{18,2},{3,19},{19,3},{4,20},{20... | collective-permute-start | bytes 589832 | tf_op jit(solution)/shard_map/ppermute | solution.py:423
  3.8 2.7 %constant_dynamic-slice_fusion.1 = bf16[2,24,128,128]{3,2,1,0:T(8,128)(2,1)} fusion(bf16[2,24,512,128]{3,2,1,0:T(8,128)(2,1)} %raw_ref.1, s32[]{:T(128)S(6)} %select_n.22), kind=kLoop, calls=%fused_computation.16 | loop fusion | bytes 3145732 | tf_op jit(solution)/shard_map/dynamic_slice | solution.py:436
  6.6 3.0 %constant_dynamic-slice_fusion = bf16[2,24,144,128]{3,2,1,0:T(8,128)(2,1)} fusion(bf16[2,24,512,128]{3,2,1,0:T(8,128)(2,1)} %raw_ref.1, s32[]{:T(128)S(6)} %select_n.21), kind=kLoop, calls=%fused_computation.15 | loop fusion | bytes 3538948 | tf_op jit(solution)/shard_map/dynamic_slice | solution.py:436
  9.6 1.5 collective-permute-start.3
  11.2 0.2 reduce-precision_reduce_fusion
  11.5 0.1 reduce_prod.9
  11.7 0.6 gather_fusion
  12.4 15.2 %shard_map.55 = (bf16[1088,288]{1,0:T(8,128)(2,1)S(1)}, bf16[256,1088]{1,0:T(8,128)(2,1)S(1)}, bf16[4,192,320]{2,1,0:T(8,128)(2,1)S(1)}, bf16[4,320,192]{2,1,0:T...) custom-call(f32[4,3,17]{2,1,0:T(4,128)S(1)} %get-tuple-element.30.ex, ...), custom_call_target="tpu_custom_call" | custom-call | bytes 30000000 | tf_op jit(solution)/shard_map/pallas_call | solution.py:460
  27.6 0.4 add_convert_fusion
  28.0 0.1 fusion
  28.1 4.5 %collective-permute-start.1 = (bf16[12,288,128]{2,1,0:T(8,128)(2,1)S(1)}, bf16[12,288,128]{2,1,0:T(8,128)(2,1)S(1)}, u32[]{:S(2)}, u32[]{:S(2)}) collective-permute-start(bf16[12,288,128]{2,1,0:T(8,128)(2,1)S(1)} %get-tuple-element.31), channel_id=1, source_target_pairs={{0,1},{1,2},{2,3},{3,4},{4,5},{5,6},{6,7},{7,8},{8,9},{9,10},{10,1... | collective-permute-start | bytes 2654216 | tf_op jit(solution)/shard_map/ppermute | solution.py:426
  32.6 1.9 %collective-permute-start.2 = (bf16[12,288,128]{2,1,0:T(8,128)(2,1)S(1)}, bf16[12,288,128]{2,1,0:T(8,128)(2,1)S(1)}, u32[]{:S(2)}, u32[]{:S(2)}) collective-permute-start(bf16[12,288,128]{2,1,0:T(8,128)(2,1)S(1)} %get-tuple-element.32), channel_id=1, source_target_pairs={{1,0},{2,1},{3,2},{4,3},{5,4},{6,5},{7,6},{8,7},{9,8},{10,9},{11,1... | collective-permute-start | bytes 2654216 | tf_op jit(solution)/shard_map/ppermute | solution.py:427
  34.7 0.1 pad_maximum_fusion.est_ref
  34.8 6.2 %shard_map.56.inner_ref = bf16[4,17,24,16,128]{4,3,2,1,0:T(8,128)(2,1)} custom-call(bf16[24,288,128]{2,1,0:T(8,128)(2,1)S(1)} %pad_maximum_fusion.est_ref, bf16[1088,288]{1,0:T(8,128)(2,1)S(1)} %get-tuple-element.17.matrix_ref), custom_call_target="tpu_custom_call" | custom-call | flops 1925185536 | bytes 8454144 | tf_op jit(solution)/shard_map/pallas_call | solution.py:216
  41.1 11.0 %collective-permute-done.1 = bf16[12,288,128]{2,1,0:T(8,128)(2,1)S(1)} collective-permute-done((bf16[12,288,128]{2,1,0:T(8,128)(2,1)S(1)}, bf16[12,288,128]{2,1,0:T(8,128)(2,1)S(1)}, u32[]{:S(2)}, u32[]{:S(2)}) %collective-permute-start.1) | collective-permute-done | bytes 884768 | tf_op jit(solution)/shard_map/ppermute | solution.py:426
  52.1 0.2 pad_maximum_fusion.1.est_ref
  52.2 6.1 %shard_map.57.outer_ref = bf16[4,17,24,16,128]{4,3,2,1,0:T(8,128)(2,1)} custom-call(bf16[24,288,128]{2,1,0:T(8,128)(2,1)S(1)} %pad_maximum_fusion.1.est_ref, bf16[1088,288]{1,0:T(8,128)(2,1)S(1)} %get-tuple-element.17.matrix_ref), custom_call_target="tpu_custom_call" | custom-call | flops 1925185536 | bytes 8454144 | tf_op jit(solution)/shard_map/pallas_call | solution.py:216
  58.4 20.2 %shard_map.58.refs_0_ = bf16[2,17,48,16,128]{4,3,2,1,0:T(8,128)(2,1)} custom-call(s32[3]{0:T(128)S(1)} %get-tuple-element.37.scalar_ref, bf16[4,17,24,16,128]{4,3,2,1,0:T(8,128)(2,1)} %shard_map.56.inner_ref, bf16[4,17,24,16,128]{4,3,2,1,0:T(8,128)(2,1)} %shard_map.57.outer_ref, bf16[2,24,512,128]{3,2,1,0:T(8,128)(2,1)} %raw_ref.1, ...), custom_call_target="tpu_custom_call" | custom-call | flops 13369344000 | bytes 16711680 | tf_op jit(solution)/shard_map/pallas_call | solution.py:320
  78.6 10.5 %shard_map.60.refs_2_ = bf16[2,8,48,16,128]{4,3,2,1,0:T(8,128)(2,1)} custom-call(s32[3]{0:T(128)S(1)} %get-tuple-element.38.scalar_ref, bf16[4,17,24,16,128]{4,3,2,1,0:T(8,128)(2,1)} %shard_map.56.inner_ref, bf16[4,17,24,16,128]{4,3,2,1,0:T(8,128)(2,1)} %shard_map.57.outer_ref, bf16[2,24,128,128]{3,2,1,0:T(8,128)(2,1)} %collective-permute-done.4.raw_ref, ...), custom_call_target="tpu_custom_call" | custom-call | flops 6291456000 | bytes 7864320 | tf_op jit(solution)/shard_map/pallas_call | solution.py:320
  89.1 12.1 %shard_map.59.refs_1_ = bf16[2,9,48,16,128]{4,3,2,1,0:T(8,128)(2,1)} custom-call(s32[3]{0:T(128)S(1)} %get-tuple-element.38.scalar_ref, bf16[4,17,24,16,128]{4,3,2,1,0:T(8,128)(2,1)} %shard_map.56.inner_ref, bf16[4,17,24,16,128]{4,3,2,1,0:T(8,128)(2,1)} %shard_map.57.outer_ref, bf16[2,24,144,128]{3,2,1,0:T(8,128)(2,1)} %collective-permute-done.3.raw_ref, ...), custom_call_target="tpu_custom_call" | custom-call | flops 7077888000 | bytes 8847360 | tf_op jit(solution)/shard_map/pallas_call | solution.py:320
  101.2 5.6 %shard_map.62 = bf16[24,256,128]{2,1,0:T(8,128)(2,1)S(1)} custom-call(bf16[2,17,48,16,128]{4,3,2,1,0:T(8,128)(2,1)} %shard_map.58.refs_0_, bf16[2,9,48,16,128]{4,3,2,1,0:T(8,128)(2,1)} %shard_map.59.refs_1_, bf16[2,8,48,16,128]{4,3,2,1,0:T(8,128)(2,1)S(1)} %copy-done.3, bf16[256,1088]{1,0:T(8,128)(2,1)S(1)} %get-tuple-element.26.refs_3_), custom_call_target="tpu_custom_call" | custom-call | flops 1711276032 | bytes 9830400 | tf_op jit(solution)/shard_map/pallas_call | solution.py:386
  106.8 0.1 fusion.6
  106.9 4.4 %collective-permute-start.5 = (bf16[12,256,128]{2,1,0:T(8,128)(2,1)S(1)}, bf16[12,256,128]{2,1,0:T(8,128)(2,1)S(1)}, u32[]{:S(2)}, u32[]{:S(2)}) collective-permute-start(bf16[12,256,128]{2,1,0:T(8,128)(2,1)S(1)} %get-tuple-element.34), channel_id=1, source_target_pairs={{0,1},{1,2},{2,3},{3,4},{4,5},{5,6},{6,7},{7,8},{8,9},{9,10},{10,1... | collective-permute-start | bytes 2359304 | tf_op jit(solution)/shard_map/ppermute | solution.py:505
  111.3 1.9 %collective-permute-start.6 = (bf16[12,256,128]{2,1,0:T(8,128)(2,1)S(1)}, bf16[12,256,128]{2,1,0:T(8,128)(2,1)S(1)}, u32[]{:S(2)}, u32[]{:S(2)}) collective-permute-start(bf16[12,256,128]{2,1,0:T(8,128)(2,1)S(1)} %get-tuple-element.33), channel_id=1, source_target_pairs={{1,0},{2,1},{3,2},{4,3},{5,4},{6,5},{7,6},{8,7},{9,8},{10,9},{11,1... | collective-permute-start | bytes 2359304 | tf_op jit(solution)/shard_map/ppermute | solution.py:506
  113.2 3.6 %collective-permute-start.7 = (s32[4,1,2]{2,1,0:T(1,128)S(1)}, s32[4,1,2]{2,1,0:T(1,128)S(1)}, u32[]{:S(2)}, u32[]{:S(2)}) collective-permute-start(s32[4,1,2]{2,1,0:T(1,128)S(1)} %copy.24.range_ref), channel_id=1, source_target_pairs={{0,1},{1,2},{2,3},{3,4},{4,5},{5,6},{6,7},{7,8},{8,9},{9,10},{10,1... | collective-permute-start | bytes 104 | tf_op jit(solution)/shard_map/ppermute | solution.py:469
  116.9 2.1 %collective-permute-start.8 = (s32[4,1,2]{2,1,0:T(1,128)S(1)}, s32[4,1,2]{2,1,0:T(1,128)S(1)}, u32[]{:S(2)}, u32[]{:S(2)}) collective-permute-start(s32[4,1,2]{2,1,0:T(1,128)S(1)} %copy.24.range_ref), channel_id=1, source_target_pairs={{1,0},{2,1},{3,2},{4,3},{5,4},{6,5},{7,6},{8,7},{9,8},{10,9},{11,1... | collective-permute-start | bytes 104 | tf_op jit(solution)/shard_map/ppermute | solution.py:470
  119.0 9.7 %collective-permute-done.7.below_ref = s32[4,1,2]{2,1,0:T(1,128)S(1)} collective-permute-done((s32[4,1,2]{2,1,0:T(1,128)S(1)}, s32[4,1,2]{2,1,0:T(1,128)S(1)}, u32[]{:S(2)}, u32[]{:S(2)}) %collective-permute-start.7) | collective-permute-done | bytes 64 | tf_op jit(solution)/shard_map/ppermute | solution.py:469
  128.7 3.2 %shard_map.63 = (f32[4,24,128]{2,1,0:T(8,128)S(1)}, f32[4,256,128]{2,1,0:T(8,128)S(1)}) custom-call(f32[4,3,17]{2,1,0:T(4,128)S(1)} %get-tuple-element.30.exact_ref, s32[4,3]{1,0:T(4,128)S(1)} %copy-done, s32[4,1,2]{2,1,0:T(1,128)S(1)} %collective-permute-done.7.below_ref, s32[4,1,2]{2,1,0:T(1,128)S(1)} %copy.24.range_ref, ...), custom_call_target="tpu_custom_call" | custom-call | bytes 8000000 | tf_op jit(solution)/shard_map/pallas_call | solution.py:471
  131.9 5.9 %shard_map.61.kept_ref = f32[24,256,128]{2,1,0:T(8,128)S(1)} custom-call(bf16[2,17,48,16,128]{4,3,2,1,0:T(8,128)(2,1)} %shard_map.58.refs_0_, bf16[2,9,48,16,128]{4,3,2,1,0:T(8,128)(2,1)} %shard_map.59.refs_1_, bf16[2,8,48,16,128]{4,3,2,1,0:T(8,128)(2,1)} %shard_map.60.refs_2_, bf16[256,1088]{1,0:T(8,128)(2,1)S(1)} %get-tuple-element.26.refs_3_), custom_call_target="tpu_custom_call" | custom-call | flops 1711276032 | bytes 9830400 | tf_op jit(solution)/shard_map/pallas_call | solution.py:386
  137.8 1.6 %copy-done.2 = f32[24,256,128]{2,1,0:T(8,128)} copy-done((f32[24,256,128]{2,1,0:T(8,128)}, f32[24,256,128]{2,1,0:T(8,128)S(1)}, u32[]{:S(2)}) %copy-start.2) | copy-done | bytes 3145752
  139.5 6.0 %shard_map.64 = f32[24,256,128]{2,1,0:T(8,128)} custom-call(f32[24,256,128]{2,1,0:T(8,128)S(1)} %copy-done.1, f32[24,256,128]{2,1,0:T(8,128)} %copy-done.2, bf16[12,256,128]{2,1,0:T(8,128)(2,1)S(1)} %collective-permute-done.5.low_ref, bf16[12,256,128]{2,1,0:T(8,128)(2,1)S(1)} %collective-permute-done.6.high_ref, f32[4,24,128]{2,1,0:T(8,128)S(1)} %get-tuple-element.27.xz_ref, ...), custom_call_target="tpu_custom_call" | custom-call | tf_op jit(solution)/shard_map/pallas_call | solution.py:509
  (29 shorter events, 0.6 us)
Async XLA Ops:
  1.7 26.2 %collective-permute-start = (bf16[24,32,128]{2,1,0:T(8,128)(2,1)}, bf16[24,32,128]{2,1,0:T(8,128)(2,1)S(1)}, u32[]{:S(2)}, u32[]{:S(2)}) collective-permute-start(bf16[24,32,128]{2,1,0:T(8,128)(2,1)} %add_convert_fusion.1), channel_id=1, source_target_pairs={{0,16},{16,0},{1,17},{17,1},{2,18},{18,2},{3,19},{19,3},{4,20},{20... | collective-permute-start | bytes 589832 | tf_op jit(solution)/shard_map/ppermute | solution.py:423
  6.5 72.1 %collective-permute-start.4 = (bf16[2,24,128,128]{3,2,1,0:T(8,128)(2,1)}, bf16[2,24,128,128]{3,2,1,0:T(8,128)(2,1)}, u32[]{:S(2)}, u32[]{:S(2)}) collective-permute-start(bf16[2,24,128,128]{3,2,1,0:T(8,128)(2,1)} %constant_dynamic-slice_fusion.1), channel_id=1, source_target_pairs={{0,16},{16,0},{1,17},{17,1},{2,18},{18,2},{3,19},{19,3},{4,20},{20... | collective-permute-start | bytes 4718600 | tf_op jit(solution)/shard_map/ppermute | solution.py:439
  6.5 4.5 %copy-start.4 = (f32[4,3,17]{2,0,1:T(4,128)S(1)}, f32[4,3,17]{2,0,1:T(4,128)}, u32[]{:S(2)}) copy-start(f32[4,3,17]{2,0,1:T(4,128)} %param.7) | copy-start | bytes 2452
  6.5 4.9 %copy-start.5 = (s32[4,1,2]{0,2,1:T(2,128)S(1)}, s32[4,1,2]{0,2,1:T(2,128)}, u32[]{:S(2)}) copy-start(s32[4,1,2]{0,2,1:T(2,128)} %param.9) | copy-start | bytes 100
  6.5 5.2 %copy-start = (s32[4,3]{1,0:T(4,128)S(1)}, s32[4,3]{1,0:T(4,128)}, u32[]{:S(2)}) copy-start(s32[4,3]{1,0:T(4,128)} %offset_ref.3) | copy-start | bytes 148
  6.5 21.0 %copy-start.1 = (f32[24,256,128]{2,1,0:T(8,128)S(1)}, f32[24,256,128]{2,1,0:T(8,128)}, u32[]{:S(2)}) copy-start(f32[24,256,128]{2,1,0:T(8,128)} %est_ref.1) | copy-start | bytes 9437188
  9.6 79.5 %collective-permute-start.3 = (bf16[2,24,144,128]{3,2,1,0:T(8,128)(2,1)}, bf16[2,24,144,128]{3,2,1,0:T(8,128)(2,1)}, u32[]{:S(2)}, u32[]{:S(2)}) collective-permute-start(bf16[2,24,144,128]{3,2,1,0:T(8,128)(2,1)} %constant_dynamic-slice_fusion), channel_id=1, source_target_pairs={{0,16},{16,0},{1,17},{17,1},{2,18},{18,2},{3,19},{19,3},{4,20},{20... | collective-permute-start | bytes 5308424 | tf_op jit(solution)/shard_map/ppermute | solution.py:439
  28.1 24.0 %collective-permute-start.1 = (bf16[12,288,128]{2,1,0:T(8,128)(2,1)S(1)}, bf16[12,288,128]{2,1,0:T(8,128)(2,1)S(1)}, u32[]{:S(2)}, u32[]{:S(2)}) collective-permute-start(bf16[12,288,128]{2,1,0:T(8,128)(2,1)S(1)} %get-tuple-element.31), channel_id=1, source_target_pairs={{0,1},{1,2},{2,3},{3,4},{4,5},{5,6},{6,7},{7,8},{8,9},{9,10},{10,1... | collective-permute-start | bytes 2654216 | tf_op jit(solution)/shard_map/ppermute | solution.py:426
  32.6 19.4 %collective-permute-start.2 = (bf16[12,288,128]{2,1,0:T(8,128)(2,1)S(1)}, bf16[12,288,128]{2,1,0:T(8,128)(2,1)S(1)}, u32[]{:S(2)}, u32[]{:S(2)}) collective-permute-start(bf16[12,288,128]{2,1,0:T(8,128)(2,1)S(1)} %get-tuple-element.32), channel_id=1, source_target_pairs={{1,0},{2,1},{3,2},{4,3},{5,4},{6,5},{7,6},{8,7},{9,8},{10,9},{11,1... | collective-permute-start | bytes 2654216 | tf_op jit(solution)/shard_map/ppermute | solution.py:427
  89.1 12.1 %copy-start.3 = (bf16[2,8,48,16,128]{4,3,2,1,0:T(8,128)(2,1)S(1)}, bf16[2,8,48,16,128]{4,3,2,1,0:T(8,128)(2,1)}, u32[]{:S(2)}) copy-start(bf16[2,8,48,16,128]{4,3,2,1,0:T(8,128)(2,1)} %shard_map.60.refs_2_) | copy-start | bytes 9437188
  106.9 32.5 %collective-permute-start.5 = (bf16[12,256,128]{2,1,0:T(8,128)(2,1)S(1)}, bf16[12,256,128]{2,1,0:T(8,128)(2,1)S(1)}, u32[]{:S(2)}, u32[]{:S(2)}) collective-permute-start(bf16[12,256,128]{2,1,0:T(8,128)(2,1)S(1)} %get-tuple-element.34), channel_id=1, source_target_pairs={{0,1},{1,2},{2,3},{3,4},{4,5},{5,6},{6,7},{7,8},{8,9},{9,10},{10,1... | collective-permute-start | bytes 2359304 | tf_op jit(solution)/shard_map/ppermute | solution.py:505
  111.3 28.1 %collective-permute-start.6 = (bf16[12,256,128]{2,1,0:T(8,128)(2,1)S(1)}, bf16[12,256,128]{2,1,0:T(8,128)(2,1)S(1)}, u32[]{:S(2)}, u32[]{:S(2)}) collective-permute-start(bf16[12,256,128]{2,1,0:T(8,128)(2,1)S(1)} %get-tuple-element.33), channel_id=1, source_target_pairs={{1,0},{2,1},{3,2},{4,3},{5,4},{6,5},{7,6},{8,7},{9,8},{10,9},{11,1... | collective-permute-start | bytes 2359304 | tf_op jit(solution)/shard_map/ppermute | solution.py:506
  113.2 15.5 %collective-permute-start.7 = (s32[4,1,2]{2,1,0:T(1,128)S(1)}, s32[4,1,2]{2,1,0:T(1,128)S(1)}, u32[]{:S(2)}, u32[]{:S(2)}) collective-permute-start(s32[4,1,2]{2,1,0:T(1,128)S(1)} %copy.24.range_ref), channel_id=1, source_target_pairs={{0,1},{1,2},{2,3},{3,4},{4,5},{5,6},{6,7},{7,8},{8,9},{9,10},{10,1... | collective-permute-start | bytes 104 | tf_op jit(solution)/shard_map/ppermute | solution.py:469
  116.9 11.8 %collective-permute-start.8 = (s32[4,1,2]{2,1,0:T(1,128)S(1)}, s32[4,1,2]{2,1,0:T(1,128)S(1)}, u32[]{:S(2)}, u32[]{:S(2)}) collective-permute-start(s32[4,1,2]{2,1,0:T(1,128)S(1)} %copy.24.range_ref), channel_id=1, source_target_pairs={{1,0},{2,1},{3,2},{4,3},{5,4},{6,5},{7,6},{8,7},{9,8},{10,9},{11,1... | collective-permute-start | bytes 104 | tf_op jit(solution)/shard_map/ppermute | solution.py:470
  137.8 1.6 %copy-start.2 = (f32[24,256,128]{2,1,0:T(8,128)}, f32[24,256,128]{2,1,0:T(8,128)S(1)}, u32[]{:S(2)}) copy-start(f32[24,256,128]{2,1,0:T(8,128)S(1)} %shard_map.61.kept_ref) | copy-start | bytes 9437188

commit v3 on v2

--- a/solution.py
+++ b/solution.py
@@ -184,17 +184,11 @@
         y_ref[w] = inside_sum(exact[1], first, -1, 0, rows_all)
 
 
-def finish_kernel(est_ref, kept_ref, low_ref, high_ref, xz_ref, y_ref, out_ref, *, sides):
-    planes = est_ref.shape[0]
-    views = y_ref.shape[0]
+def finish_kernel(kept_ref, factor_ref, low_ref, high_ref, out_ref, *, sides):
     step = pl.program_id(0)
     is_low = jnp.where(step < sides, 1.0, 0.0)
-    for plane in range(planes):
-        at = pl.ds(step * planes + plane, 1)
-        weight = sum(y_ref[w] * xz_ref[w, at] for w in range(views))
-        edge = low_ref[plane].astype(F32) * is_low + high_ref[plane].astype(F32) * (1.0 - is_low)
-        correction = kept_ref[plane] + edge + QUO_MID * weight
-        out_ref[plane] = est_ref[plane] * correction / jnp.maximum(weight, FLOOR)
+    edge = low_ref[...].astype(F32) * is_low + high_ref[...].astype(F32) * (1.0 - is_low)
+    out_ref[...] = factor_ref[...] * (kept_ref[...] + edge)
 
 
 def rows_forward_kernel(est_ref, matrix_ref, out_ref):
@@ -350,10 +344,14 @@
     )(scalars, inner, outer, raw, plane, plane_t, depth_m, depth_mt, ones_x, ones_yz, cover, scale)
 
 
-def rows_back_kernel(*refs):
-    *part_refs, matrix_ref, out_ref = refs
+def rows_back_kernel(*refs, weighted):
+    if weighted:
+        *part_refs, matrix_ref, est_ref, xz_ref, y_ref, out_ref, factor_ref = refs
+    else:
+        *part_refs, matrix_ref, out_ref = refs
     own_ref, *other_refs = part_refs
     planes, _, depth = out_ref.shape
+    step = pl.program_id(0)
 
     def rows_of(ref, slot, plane):
         return ref[slot, :, plane].reshape(ref.shape[1] * ROWS, depth)
@@ -369,12 +367,17 @@
                         )
                     )
         data = jnp.concatenate(pieces, axis=0)
-        done = jnp.dot(matrix_ref[...], data, preferred_element_type=F32).astype(out_ref.dtype)
-        out_ref[pair] = done[:, :depth]
-        out_ref[pair + 1] = done[:, depth:]
-
-
-def rows_back(parts, matrix, blocks, place, dtype):
+        done = jnp.dot(matrix_ref[...], data, preferred_element_type=F32)
+        for plane, part in ((pair, done[:, :depth]), (pair + 1, done[:, depth:])):
+            if weighted:
+                at = pl.ds(step * planes + plane, 1)
+                weight = sum(y_ref[w] * xz_ref[w, at] for w in range(y_ref.shape[0]))
+                part = part + QUO_MID * weight
+                factor_ref[plane] = est_ref[plane] / jnp.maximum(weight, FLOOR)
+            out_ref[plane] = part.astype(out_ref.dtype)
+
+
+def rows_back(parts, matrix, blocks, place, weighted=None):
     depth = parts[0].shape[-1]
     rows_out = matrix.shape[0]
 
@@ -383,20 +386,31 @@
             part.shape[:2] + (PLANES, ROWS, depth), lambda i: (0, 0, place(i), 0, 0)
         )
 
+    block_spec = pl.BlockSpec((PLANES, rows_out, depth), lambda i: (i, 0, 0))
+    in_specs = [planes_of(part) for part in parts]
+    in_specs.append(pl.BlockSpec(matrix.shape, lambda i: (0, 0)))
+    shape = (blocks * PLANES, rows_out, depth)
+    out_specs, out_shape, extra = block_spec, jax.ShapeDtypeStruct(shape, BF16), ()
+    if weighted is not None:
+        extra = weighted
+        in_specs.append(block_spec)
+        in_specs += [pl.BlockSpec(table.shape, lambda i: (0, 0, 0)) for table in extra[1:]]
+        out_specs = [block_spec] * 2
+        out_shape = [jax.ShapeDtypeStruct(shape, F32)] * 2
+
     return pl.pallas_call(
-        rows_back_kernel,
+        functools.partial(rows_back_kernel, weighted=weighted is not None),
         grid=(blocks,),
-        in_specs=[planes_of(part) for part in parts]
-        + [pl.BlockSpec(matrix.shape, lambda i: (0, 0))],
-        out_specs=pl.BlockSpec((PLANES, rows_out, depth), lambda i: (i, 0, 0)),
-        out_shape=jax.ShapeDtypeStruct((blocks * PLANES, rows_out, depth), dtype),
+        in_specs=in_specs,
+        out_specs=out_specs,
+        out_shape=out_shape,
         compiler_params=pltpu.CompilerParams(vmem_limit_bytes=VMEM_LIMIT),
         cost_estimate=pl.CostEstimate(
             flops=2 * blocks * PLANES * depth * matrix.size,
             bytes_accessed=2 * blocks * PLANES * depth * (matrix.shape[1] + 2 * rows_out),
             transcendentals=0,
         ),
-    )(*parts, matrix)
+    )(*parts, matrix, *extra)
 
 
 def on_device(estimate, raw_tiles, psf_taps, view_offsets, depth_range):
@@ -418,9 +432,30 @@
 
     start = (1 - place) * (half_rows - est_extra)
     edge = lax.dynamic_slice_in_dim(estimate, start, est_extra, 1)
-    edge = (edge - EST_MID).astype(BF16)
+    edge = lax.ppermute((edge - EST_MID).astype(BF16), "view", swap)
     centred = (estimate - EST_MID).astype(BF16)
-    inner_est = jnp.concatenate([centred, lax.ppermute(edge, "view", swap)], axis=1)
+    inner_est = jnp.concatenate([centred, edge], axis=1)
+
+    other_start = (1 - place) * (half_rows - ROWS)
+    cuts = [0, groups - groups // 4, groups]
+    arrived = []
+    for low, high in zip(cuts, cuts[1:]):
+        if low > 0:
+            other_start, edge = lax.optimization_barrier((other_start, edge))
+        piece = lax.dynamic_slice_in_dim(
+            raw_tiles, other_start + low * ROWS, (high - low) * ROWS, 2
+        )
+        arrived.append(lax.ppermute(piece, "view", swap))
+
+    kernels = psf_taps / jnp.sum(psf_taps, axis=2, keepdims=True)
+    rounded = lax.reduce_precision(kernels, 8, 7)
+    scale = 1.0 / jnp.prod(jnp.sum(rounded, axis=2), axis=1)
+    position = jnp.stack([place, lax.axis_index("tile")]).astype(jnp.int32)
+
+    position, inner_est = lax.optimization_barrier((position, inner_est))
+    below = lax.ppermute(depth_range, "tile", up)
+    above = lax.ppermute(depth_range, "tile", down)
+
     outer_est = jnp.concatenate(
         [
             lax.ppermute(inner_est[block - halo :], "tile", up),
@@ -428,20 +463,6 @@
         ],
         axis=0,
     )
-
-    other_start = (1 - place) * (half_rows - ROWS)
-    cuts = [0, (groups + 1) // 2, groups]
-    arrived = []
-    for low, high in zip(cuts, cuts[1:]):
-        piece = lax.dynamic_slice_in_dim(
-            raw_tiles, other_start + low * ROWS, (high - low) * ROWS, 2
-        )
-        arrived.append(lax.ppermute(piece, "view", swap))
-
-    kernels = psf_taps / jnp.sum(psf_taps, axis=2, keepdims=True)
-    rounded = lax.reduce_precision(kernels, 8, 7)
-    scale = 1.0 / jnp.prod(jnp.sum(rounded, axis=2), axis=1)
-    position = jnp.stack([place, lax.axis_index("tile")]).astype(jnp.int32)
 
     smem = pl.BlockSpec(memory_space=pltpu.SMEM)
     vmem = pl.BlockSpec(memory_space=pltpu.VMEM)
@@ -466,8 +487,6 @@
         cost_estimate=pl.CostEstimate(flops=0, bytes_accessed=30_000_000, transcendentals=0),
     )(kernels, rounded, scale, view_offsets, depth_range, position)
 
-    below = lax.ppermute(depth_range, "tile", up)
-    above = lax.ppermute(depth_range, "tile", down)
     table_xz, table_y = pl.pallas_call(
         functools.partial(weight_tables_kernel, rows_all=rows_all),
         in_specs=[smem] * 6,
@@ -485,11 +504,13 @@
     own_first = lax.rem(place * slots + jnp.arange(views), views)
     starts = view_offsets[own_first, 0] + (halo - half)
     base = place * ((half_rows - ROWS) // ROWS)
+    base, table_xz, table_y = lax.optimization_barrier((base, table_xz, table_y))
     zero = jnp.zeros((), jnp.int32)
     parts = [
         view_pass(0, slots, 0, groups, base, starts[:slots], inner, outer, raw_tiles, tables)
     ]
     for low, high, piece in zip(cuts, cuts[1:], arrived):
+        zero, parts[-1] = lax.optimization_barrier((zero, parts[-1]))
         parts.append(
             view_pass(
                 1, slots, low, high - low, zero, starts[slots:], inner, outer, piece, tables
@@ -499,28 +520,29 @@
     side = halo // PLANES
     middle = block // PLANES
     edges = rows_back(
-        parts, rows_mt, 2 * side, lambda i: jnp.where(i < side, i, i + middle), BF16
+        parts, rows_mt, 2 * side, lambda i: jnp.where(i < side, i, i + middle)
     )
-    kept = rows_back(parts, rows_mt, middle, lambda i: i + side, F32)
     low = lax.ppermute(edges[halo:], "tile", up)
     high = lax.ppermute(edges[:halo], "tile", down)
-    sides = halo // PLANES
-    whole = (PLANES, half_rows, depth)
+    kept, factor = rows_back(
+        parts, rows_mt, middle, lambda i: i + side, (estimate, table_xz, table_y)
+    )
+    step = 2
+    sides = halo // step
+    whole = pl.BlockSpec((step, half_rows, depth), lambda i: (i, 0, 0))
     return pl.pallas_call(
         functools.partial(finish_kernel, sides=sides),
-        grid=(middle,),
+        grid=(block // step,),
         in_specs=[
-            pl.BlockSpec(whole, lambda i: (i, 0, 0)),
-            pl.BlockSpec(whole, lambda i: (i, 0, 0)),
-            pl.BlockSpec(whole, lambda i: (jnp.minimum(i, sides - 1), 0, 0)),
-            pl.BlockSpec(whole, lambda i: (jnp.maximum(i - sides, 0), 0, 0)),
-            pl.BlockSpec(table_xz.shape, lambda i: (0, 0, 0)),
-            pl.BlockSpec(table_y.shape, lambda i: (0, 0, 0)),
+            whole,
+            whole,
+            pl.BlockSpec(whole.block_shape, lambda i: (jnp.minimum(i, sides - 1), 0, 0)),
+            pl.BlockSpec(whole.block_shape, lambda i: (jnp.maximum(i - sides, 0), 0, 0)),
         ],
-        out_specs=pl.BlockSpec(whole, lambda i: (i, 0, 0)),
+        out_specs=whole,
         out_shape=jax.ShapeDtypeStruct(estimate.shape, F32),
         compiler_params=pltpu.CompilerParams(vmem_limit_bytes=VMEM_LIMIT),
-    )(estimate, kept, low, high, table_xz, table_y)
+    )(kept, factor, low, high)
 
 
 def solution(mesh):

time: 147 us -> 139 us (0.946)
  the two profiles are of different devices: /device:TPU:1 before, /device:TPU:25 now
where the time goes in v3:
time: 139 us; the launch traced here: 138 us
  Pallas kernels  94.2 us (68%)
  starting transfers between devices  19.2 us (14%)
  waiting for transfers between devices  9.97 us (7%)
  local copies, waits for them, and re-layouts  8.03 us (6%)
  other arithmetic  6.13 us (4%)
    pallas_call x3, Pallas kernels, view_pass(): pl.pallas_call(view_kernel, grid_spec=pltpu.PrefetchScalarGridSpec(num_sc...  41.6 us
    pallas_call x1, Pallas kernels, on_device(): pl.pallas_call(functools.partial(tables_kernel, slots=slots, tiles=tiles,...  15.2 us
    pallas_call x2, Pallas kernels, rows_back(): pl.pallas_call(functools.partial(rows_back_kernel, weighted=weighted is n...  13.7 us
    pallas_call x2, Pallas kernels, rows_forward(): pl.pallas_call(rows_forward_kernel, grid=(count // PLANES,), in_specs=[pl...  12.4 us
    ppermute x1, waiting for transfers between devices, on_device(): high = lax.ppermute(edges[:halo], 'tile', down)  9.95 us
    pallas_call x1, Pallas kernels, on_device(): pl.pallas_call(functools.partial(finish_kernel, sides=sides), grid=(block...  8.13 us
    dynamic_slice x2, local copies, waits for them, and re-layouts, on_device(): lax.dynamic_slice_in_dim(raw_tiles, other_start + low * ROWS, (high - low...  4.93 us
    ppermute x1, starting transfers between devices, on_device(): lax.ppermute(inner_est[:halo], 'tile', down)  3.99 us
  transfers between devices with their start and end apart: 9, of which 1 were waited for; matrix products, arithmetic and copies ran while one was open for 10% of the time, Pallas kernels for 54%

profile of v3, /device:TPU:25, one launch (start us, length us, event | category | flops | bytes accessed | tf_op | source)
XLA Modules:
  0.0 137.7 jit_solution(13458572767282977362)
XLA Ops:
  0.0 0.8 copy.24.range_ref
  0.8 3.7 %collective-permute-start = (s32[4,1,2]{2,1,0:T(1,128)S(1)}, s32[4,1,2]{2,1,0:T(1,128)S(1)}, u32[]{:S(2)}, u32[]{:S(2)}) collective-permute-start(s32[4,1,2]{2,1,0:T(1,128)S(1)} %copy.24.range_ref), channel_id=1, source_target_pairs={{0,1},{1,2},{2,3},{3,4},{4,5},{5,6},{6,7},{7,8},{8,9},{9,10},{10,1... | collective-permute-start | bytes 104 | tf_op jit(solution)/shard_map/ppermute | solution.py:456
  4.4 1.9 %collective-permute-start.1 = (s32[4,1,2]{2,1,0:T(1,128)S(1)}, s32[4,1,2]{2,1,0:T(1,128)S(1)}, u32[]{:S(2)}, u32[]{:S(2)}) collective-permute-start(s32[4,1,2]{2,1,0:T(1,128)S(1)} %copy.24.range_ref), channel_id=1, source_target_pairs={{1,0},{2,1},{3,2},{4,3},{5,4},{6,5},{7,6},{8,7},{9,8},{10,9},{11,1... | collective-permute-start | bytes 104 | tf_op jit(solution)/shard_map/ppermute | solution.py:457
  6.4 1.0 add_convert_fusion.1
  7.4 1.3 collective-permute-start.2
  8.7 3.5 %constant_dynamic-slice_fusion = bf16[2,24,208,128]{3,2,1,0:T(8,128)(2,1)} fusion(bf16[2,24,512,128]{3,2,1,0:T(8,128)(2,1)} %raw_ref.1, s32[]{:T(128)S(6)} %select_n.21), kind=kLoop, calls=%fused_computation.9 | loop fusion | bytes 5111812 | tf_op jit(solution)/shard_map/dynamic_slice | solution.py:445
  12.2 0.2 collective-permute-start.5
  12.5 1.5 %add_convert_fusion = bf16[24,256,128]{2,1,0:T(8,128)(2,1)} fusion(f32[24,256,128]{2,1,0:T(8,128)S(1)} %copy-done.1), kind=kLoop, calls=%fused_computation.1 | loop fusion | flops 1572864 | bytes 4718592 | tf_op jit(solution)/shard_map/convert_element_type | solution.py:436
  14.2 0.6 gather_fusion
  14.9 0.2 reduce-precision_reduce_fusion
  15.1 1.5 %pad_maximum_fusion.est_ref = bf16[24,288,128]{2,1,0:T(8,128)(2,1)S(1)} fusion(bf16[24,32,128]{2,1,0:T(8,128)(2,1)S(1)} %collective-permute-done.2, bf16[24,256,128]{2,1,0:T(8,128)(2,1)} %add_convert_fusion), kind=kLoop, calls=%fused_computation.2 | loop fusion | flops 3538944 | bytes 3538944 | tf_op jit(solution)/shard_map/concatenate | solution.py:437
  16.6 1.4 fusion.4
  18.0 4.0 %collective-permute-start.4 = (bf16[12,288,128]{2,1,0:T(8,128)(2,1)}, bf16[12,288,128]{2,1,0:T(8,128)(2,1)S(1)}, u32[]{:S(2)}, u32[]{:S(2)}) collective-permute-start(bf16[12,288,128]{2,1,0:T(8,128)(2,1)} %get-tuple-element.56), channel_id=1, source_target_pairs={{1,0},{2,1},{3,2},{4,3},{5,4},{6,5},{7,6},{8,7},{9,8},{10,9},{11,1... | collective-permute-start | bytes 2654216 | tf_op jit(solution)/shard_map/ppermute | solution.py:462
  22.0 2.1 %collective-permute-start.3 = (bf16[12,288,128]{2,1,0:T(8,128)(2,1)}, bf16[12,288,128]{2,1,0:T(8,128)(2,1)}, u32[]{:S(2)}, u32[]{:S(2)}) collective-permute-start(bf16[12,288,128]{2,1,0:T(8,128)(2,1)} %get-tuple-element.55), channel_id=1, source_target_pairs={{0,1},{1,2},{2,3},{3,4},{4,5},{5,6},{6,7},{7,8},{8,9},{9,10},{10,1... | collective-permute-start | bytes 2654216 | tf_op jit(solution)/shard_map/ppermute | solution.py:461
  24.2 0.1 reduce_prod.9
  24.4 3.2 %shard_map.55 = (f32[4,24,128]{2,1,0:T(8,128)S(1)}, f32[4,256,128]{2,1,0:T(8,128)S(1)}) custom-call(f32[4,3,17]{2,1,0:T(4,128)S(1)} %get-tuple-element.54.exact_ref, s32[4,3]{1,0:T(4,128)S(1)} %copy-done, s32[4,1,2]{2,1,0:T(1,128)S(1)} %collective-permute-done.below_ref, s32[4,1,2]{2,1,0:T(1,128)S(1)} %copy.24.range_ref, ...), custom_call_target="tpu_custom_call" | custom-call | bytes 8000000 | tf_op jit(solution)/shard_map/pallas_call | solution.py:490
  27.6 1.4 %constant_dynamic-slice_fusion.1 = bf16[2,24,64,128]{3,2,1,0:T(8,128)(2,1)S(1)} fusion(bf16[2,24,512,128]{3,2,1,0:T(8,128)(2,1)} %raw_ref.1, s32[]{:T(128)S(6)} %select_n.22), kind=kLoop, calls=%fused_computation.10 | loop fusion | bytes 1572868 | tf_op jit(solution)/shard_map/dynamic_slice | solution.py:445
  29.0 1.3 collective-permute-start.6
  30.4 15.2 %shard_map.56 = (bf16[1088,288]{1,0:T(8,128)(2,1)S(1)}, bf16[256,1088]{1,0:T(8,128)(2,1)S(1)}, bf16[4,192,320]{2,1,0:T(8,128)(2,1)S(1)}, bf16[4,320,192]{2,1,0:T...) custom-call(f32[4,3,17]{2,1,0:T(4,128)S(1)} %get-tuple-element.54.ex, ...), custom_call_target="tpu_custom_call" | custom-call | bytes 30000000 | tf_op jit(solution)/shard_map/pallas_call | solution.py:481
  45.6 6.2 %shard_map.57.inner_ref = bf16[4,17,24,16,128]{4,3,2,1,0:T(8,128)(2,1)} custom-call(bf16[24,288,128]{2,1,0:T(8,128)(2,1)S(1)} %pad_maximum_fusion.est_ref, bf16[1088,288]{1,0:T(8,128)(2,1)S(1)} %get-tuple-element.34.matrix_ref), custom_call_target="tpu_custom_call" | custom-call | flops 1925185536 | bytes 8454144 | tf_op jit(solution)/shard_map/pallas_call | solution.py:210
  51.8 1.3 pad_maximum_fusion.1.est_ref
  53.2 6.2 %shard_map.58.outer_ref = bf16[4,17,24,16,128]{4,3,2,1,0:T(8,128)(2,1)} custom-call(bf16[24,288,128]{2,1,0:T(8,128)(2,1)S(1)} %pad_maximum_fusion.1.est_ref, bf16[1088,288]{1,0:T(8,128)(2,1)S(1)} %get-tuple-element.34.matrix_ref), custom_call_target="tpu_custom_call" | custom-call | flops 1925185536 | bytes 8454144 | tf_op jit(solution)/shard_map/pallas_call | solution.py:210
  59.3 20.2 %shard_map.59.refs_0_ = bf16[2,17,48,16,128]{4,3,2,1,0:T(8,128)(2,1)} custom-call(s32[3]{0:T(128)S(1)} %pad_add_fusion.1.scalar_ref, bf16[4,17,24,16,128]{4,3,2,1,0:T(8,128)(2,1)} %shard_map.57.inner_ref, bf16[4,17,24,16,128]{4,3,2,1,0:T(8,128)(2,1)} %shard_map.58.outer_ref, bf16[2,24,512,128]{3,2,1,0:T(8,128)(2,1)} %raw_ref.1, ...), custom_call_target="tpu_custom_call" | custom-call | flops 13369344000 | bytes 16711680 | tf_op jit(solution)/shard_map/pallas_call | solution.py:314
  79.6 16.0 %shard_map.60.refs_1_ = bf16[2,13,48,16,128]{4,3,2,1,0:T(8,128)(2,1)} custom-call(s32[3]{0:T(128)S(1)} %pad_add_fusion.2.scalar_ref, bf16[4,17,24,16,128]{4,3,2,1,0:T(8,128)(2,1)} %shard_map.57.inner_ref, bf16[4,17,24,16,128]{4,3,2,1,0:T(8,128)(2,1)} %shard_map.58.outer_ref, bf16[2,24,208,128]{3,2,1,0:T(8,128)(2,1)} %collective-permute-done.5.raw_ref, ...), custom_call_target="tpu_custom_call" | custom-call | flops 10223616000 | bytes 12779520 | tf_op jit(solution)/shard_map/pallas_call | solution.py:314
  95.8 5.3 %shard_map.61.refs_2_ = bf16[2,4,48,16,128]{4,3,2,1,0:T(8,128)(2,1)S(1)} custom-call(s32[3]{0:T(128)S(1)} %pad_add_fusion.3.scalar_ref, bf16[4,17,24,16,128]{4,3,2,1,0:T(8,128)(2,1)} %shard_map.57.inner_ref, bf16[4,17,24,16,128]{4,3,2,1,0:T(8,128)(2,1)} %shard_map.58.outer_ref, bf16[2,24,64,128]{3,2,1,0:T(8,128)(2,1)S(1)} %collective-permute-done.6.raw_ref, ...), custom_call_target="tpu_custom_call" | custom-call | flops 3145728000 | bytes 3932160 | tf_op jit(solution)/shard_map/pallas_call | solution.py:314
  101.1 5.8 %shard_map.63 = bf16[24,256,128]{2,1,0:T(8,128)(2,1)S(1)} custom-call(bf16[2,17,48,16,128]{4,3,2,1,0:T(8,128)(2,1)} %shard_map.59.refs_0_, bf16[2,13,48,16,128]{4,3,2,1,0:T(8,128)(2,1)} %shard_map.60.refs_1_, bf16[2,4,48,16,128]{4,3,2,1,0:T(8,128)(2,1)S(1)} %shard_map.61.refs_2_, bf16[256,1088]{1,0:T(8,128)(2,1)S(1)} %get-tuple-element.48.refs_3_), custom_call_target="tpu_custom_call" | custom-call | flops 1711276032 | bytes 9830400 | tf_op jit(solution)/shard_map/pallas_call | solution.py:401
  106.9 0.1 fusion.5
  107.1 2.7 %collective-permute-start.7 = (bf16[12,256,128]{2,1,0:T(8,128)(2,1)S(1)}, bf16[12,256,128]{2,1,0:T(8,128)(2,1)S(1)}, u32[]{:S(2)}, u32[]{:S(2)}) collective-permute-start(bf16[12,256,128]{2,1,0:T(8,128)(2,1)S(1)} %get-tuple-element.58), channel_id=1, source_target_pairs={{0,1},{1,2},{2,3},{3,4},{4,5},{5,6},{6,7},{7,8},{8,9},{9,10},{10,1... | collective-permute-start | bytes 2359304 | tf_op jit(solution)/shard_map/ppermute | solution.py:525
  109.8 1.9 %collective-permute-start.8 = (bf16[12,256,128]{2,1,0:T(8,128)(2,1)S(1)}, bf16[12,256,128]{2,1,0:T(8,128)(2,1)S(1)}, u32[]{:S(2)}, u32[]{:S(2)}) collective-permute-start(bf16[12,256,128]{2,1,0:T(8,128)(2,1)S(1)} %get-tuple-element.57), channel_id=1, source_target_pairs={{1,0},{2,1},{3,2},{4,3},{5,4},{6,5},{7,6},{8,7},{9,8},{10,9},{11,1... | collective-permute-start | bytes 2359304 | tf_op jit(solution)/shard_map/ppermute | solution.py:526
  111.8 7.9 %shard_map.62 = (f32[24,256,128]{2,1,0:T(8,128)S(1)}, f32[24,256,128]{2,1,0:T(8,128)}) custom-call(bf16[2,17,48,16,128]{4,3,2,1,0:T(8,128)(2,1)} %shard_map.59.refs_0_, bf16[2,13,48,16,128]{4,3,2,1,0:T(8,128)(2,1)} %shard_map.60.refs_1_, bf16[2,4,48,16,128]{4,3,2,1,0:T(8,128)(2,1)S(1)} %shard_map.61.refs_2_, ...), custom_call_target="tpu_custom_call" | custom-call | flops 1711276032 | bytes 9830400 | tf_op jit(solution)/shard_map/pallas_call | solution.py:401
  119.7 9.9 %collective-permute-done.8.high_ref = bf16[12,256,128]{2,1,0:T(8,128)(2,1)S(1)} collective-permute-done((bf16[12,256,128]{2,1,0:T(8,128)(2,1)S(1)}, bf16[12,256,128]{2,1,0:T(8,128)(2,1)S(1)}, u32[]{:S(2)}, u32[]{:S(2)}) %collective-permute-start.8) | collective-permute-done | bytes 786464 | tf_op jit(solution)/shard_map/ppermute | solution.py:526
  129.6 8.1 %shard_map.64 = f32[24,256,128]{2,1,0:T(8,128)} custom-call(f32[24,256,128]{2,1,0:T(8,128)S(1)} %get-tuple-element.51.kept_ref, f32[24,256,128]{2,1,0:T(8,128)} %get-tuple-element.52.factor_ref, bf16[12,256,128]{2,1,0:T(8,128)(2,1)S(1)} %collective-permute-done.7.low_ref, bf16[12,256,128]{2,1,0:T(8,128)(2,1)S(1)} %collective-permute-done.8.high_ref), custom_call_target="tpu_custom_call" | custom-call | tf_op jit(solution)/shard_map/pallas_call | solution.py:533
  (25 shorter events, 0.6 us)
Async XLA Ops:
  0.8 23.6 %collective-permute-start = (s32[4,1,2]{2,1,0:T(1,128)S(1)}, s32[4,1,2]{2,1,0:T(1,128)S(1)}, u32[]{:S(2)}, u32[]{:S(2)}) collective-permute-start(s32[4,1,2]{2,1,0:T(1,128)S(1)} %copy.24.range_ref), channel_id=1, source_target_pairs={{0,1},{1,2},{2,3},{3,4},{4,5},{5,6},{6,7},{7,8},{8,9},{9,10},{10,1... | collective-permute-start | bytes 104 | tf_op jit(solution)/shard_map/ppermute | solution.py:456
  4.4 19.9 %collective-permute-start.1 = (s32[4,1,2]{2,1,0:T(1,128)S(1)}, s32[4,1,2]{2,1,0:T(1,128)S(1)}, u32[]{:S(2)}, u32[]{:S(2)}) collective-permute-start(s32[4,1,2]{2,1,0:T(1,128)S(1)} %copy.24.range_ref), channel_id=1, source_target_pairs={{1,0},{2,1},{3,2},{4,3},{5,4},{6,5},{7,6},{8,7},{9,8},{10,9},{11,1... | collective-permute-start | bytes 104 | tf_op jit(solution)/shard_map/ppermute | solution.py:457
  7.4 7.7 %collective-permute-start.2 = (bf16[24,32,128]{2,1,0:T(8,128)(2,1)S(1)}, bf16[24,32,128]{2,1,0:T(8,128)(2,1)S(1)}, u32[]{:S(2)}, u32[]{:S(2)}) collective-permute-start(bf16[24,32,128]{2,1,0:T(8,128)(2,1)S(1)} %add_convert_fusion.1), channel_id=1, source_target_pairs={{0,16},{16,0},{1,17},{17,1},{2,18},{18,2},{3,19},{19,3},{4,20},{20... | collective-permute-start | bytes 589832 | tf_op jit(solution)/shard_map/ppermute | solution.py:435
  8.7 3.7 %copy-start.1 = (f32[24,256,128]{2,1,0:T(8,128)S(1)}, f32[24,256,128]{2,1,0:T(8,128)}, u32[]{:S(2)}) copy-start(f32[24,256,128]{2,1,0:T(8,128)} %refs_4_.1) | copy-start | bytes 9437188
  12.2 1.8 %copy-start.2 = (f32[4,3,17]{2,0,1:T(4,128)S(1)}, f32[4,3,17]{2,0,1:T(4,128)}, u32[]{:S(2)}) copy-start(f32[4,3,17]{2,0,1:T(4,128)} %param.7) | copy-start | bytes 2452
  12.2 2.0 %copy-start = (s32[4,3]{1,0:T(4,128)S(1)}, s32[4,3]{1,0:T(4,128)}, u32[]{:S(2)}) copy-start(s32[4,3]{1,0:T(4,128)} %offset_ref.3) | copy-start | bytes 148
  12.2 67.4 %collective-permute-start.5 = (bf16[2,24,208,128]{3,2,1,0:T(8,128)(2,1)}, bf16[2,24,208,128]{3,2,1,0:T(8,128)(2,1)}, u32[]{:S(2)}, u32[]{:S(2)}) collective-permute-start(bf16[2,24,208,128]{3,2,1,0:T(8,128)(2,1)} %constant_dynamic-slice_fusion), channel_id=1, source_target_pairs={{0,16},{16,0},{1,17},{17,1},{2,18},{18,2},{3,19},{19,3},{4,20},{20... | collective-permute-start | bytes 7667720 | tf_op jit(solution)/shard_map/ppermute | solution.py:448
  18.0 33.8 %collective-permute-start.4 = (bf16[12,288,128]{2,1,0:T(8,128)(2,1)}, bf16[12,288,128]{2,1,0:T(8,128)(2,1)S(1)}, u32[]{:S(2)}, u32[]{:S(2)}) collective-permute-start(bf16[12,288,128]{2,1,0:T(8,128)(2,1)} %get-tuple-element.56), channel_id=1, source_target_pairs={{1,0},{2,1},{3,2},{4,3},{5,4},{6,5},{7,6},{8,7},{9,8},{10,9},{11,1... | collective-permute-start | bytes 2654216 | tf_op jit(solution)/shard_map/ppermute | solution.py:462
  22.0 29.8 %collective-permute-start.3 = (bf16[12,288,128]{2,1,0:T(8,128)(2,1)}, bf16[12,288,128]{2,1,0:T(8,128)(2,1)}, u32[]{:S(2)}, u32[]{:S(2)}) collective-permute-start(bf16[12,288,128]{2,1,0:T(8,128)(2,1)} %get-tuple-element.55), channel_id=1, source_target_pairs={{0,1},{1,2},{2,3},{3,4},{4,5},{5,6},{6,7},{7,8},{8,9},{9,10},{10,1... | collective-permute-start | bytes 2654216 | tf_op jit(solution)/shard_map/ppermute | solution.py:461
  29.0 66.7 %collective-permute-start.6 = (bf16[2,24,64,128]{3,2,1,0:T(8,128)(2,1)S(1)}, bf16[2,24,64,128]{3,2,1,0:T(8,128)(2,1)S(1)}, u32[]{:S(2)}, u32[]{:S(2)}) collective-permute-start(bf16[2,24,64,128]{3,2,1,0:T(8,128)(2,1)S(1)} %constant_dynamic-slice_fusion.1), channel_id=1, source_target_pairs={{0,16},{16,0},{1,17},{17,1},{2,18},{18,2},{3,19},{19,3},{4,20},{20... | collective-permute-start | bytes 2359304 | tf_op jit(solution)/shard_map/ppermute | solution.py:448
  107.1 12.6 %collective-permute-start.7 = (bf16[12,256,128]{2,1,0:T(8,128)(2,1)S(1)}, bf16[12,256,128]{2,1,0:T(8,128)(2,1)S(1)}, u32[]{:S(2)}, u32[]{:S(2)}) collective-permute-start(bf16[12,256,128]{2,1,0:T(8,128)(2,1)S(1)} %get-tuple-element.58), channel_id=1, source_target_pairs={{0,1},{1,2},{2,3},{3,4},{4,5},{5,6},{6,7},{7,8},{8,9},{9,10},{10,1... | collective-permute-start | bytes 2359304 | tf_op jit(solution)/shard_map/ppermute | solution.py:525
  109.8 19.8 %collective-permute-start.8 = (bf16[12,256,128]{2,1,0:T(8,128)(2,1)S(1)}, bf16[12,256,128]{2,1,0:T(8,128)(2,1)S(1)}, u32[]{:S(2)}, u32[]{:S(2)}) collective-permute-start(bf16[12,256,128]{2,1,0:T(8,128)(2,1)S(1)} %get-tuple-element.57), channel_id=1, source_target_pairs={{1,0},{2,1},{3,2},{4,3},{5,4},{6,5},{7,6},{8,7},{9,8},{10,9},{11,1... | collective-permute-start | bytes 2359304 | tf_op jit(solution)/shard_map/ppermute | solution.py:526

commit v4 on v2

--- a/solution.py
+++ b/solution.py
@@ -21,9 +21,11 @@
 
 
 def banded(taps, number):
-    total = jnp.zeros(number.shape, F32)
+    number = number.astype(F32).astype(BF16)
+    total = jnp.zeros(number.shape, BF16)
     for index, tap in enumerate(taps):
-        total = jnp.where(number == index, tap, total)
+        value = jnp.full(number.shape, tap, F32).astype(BF16)
+        total = jnp.where(number == jnp.array(index, BF16), value, total)
     return total
 
 
@@ -184,19 +186,6 @@
         y_ref[w] = inside_sum(exact[1], first, -1, 0, rows_all)
 
 
-def finish_kernel(est_ref, kept_ref, low_ref, high_ref, xz_ref, y_ref, out_ref, *, sides):
-    planes = est_ref.shape[0]
-    views = y_ref.shape[0]
-    step = pl.program_id(0)
-    is_low = jnp.where(step < sides, 1.0, 0.0)
-    for plane in range(planes):
-        at = pl.ds(step * planes + plane, 1)
-        weight = sum(y_ref[w] * xz_ref[w, at] for w in range(views))
-        edge = low_ref[plane].astype(F32) * is_low + high_ref[plane].astype(F32) * (1.0 - is_low)
-        correction = kept_ref[plane] + edge + QUO_MID * weight
-        out_ref[plane] = est_ref[plane] * correction / jnp.maximum(weight, FLOOR)
-
-
 def rows_forward_kernel(est_ref, matrix_ref, out_ref):
     views, groups, planes, _, depth = out_ref.shape
     rows = groups * ROWS
@@ -369,7 +358,8 @@
                         )
                     )
         data = jnp.concatenate(pieces, axis=0)
-        done = jnp.dot(matrix_ref[...], data, preferred_element_type=F32).astype(out_ref.dtype)
+        done = jnp.dot(matrix_ref[...], data, preferred_element_type=F32)
+        done = done.astype(out_ref.dtype)
         out_ref[pair] = done[:, :depth]
         out_ref[pair + 1] = done[:, depth:]
 
@@ -383,13 +373,16 @@
             part.shape[:2] + (PLANES, ROWS, depth), lambda i: (0, 0, place(i), 0, 0)
         )
 
+    block_spec = pl.BlockSpec((PLANES, rows_out, depth), lambda i: (i, 0, 0))
+    in_specs = [planes_of(part) for part in parts]
+    in_specs.append(pl.BlockSpec(matrix.shape, lambda i: (0, 0)))
+    shape = (blocks * PLANES, rows_out, depth)
     return pl.pallas_call(
         rows_back_kernel,
         grid=(blocks,),
-        in_specs=[planes_of(part) for part in parts]
-        + [pl.BlockSpec(matrix.shape, lambda i: (0, 0))],
-        out_specs=pl.BlockSpec((PLANES, rows_out, depth), lambda i: (i, 0, 0)),
-        out_shape=jax.ShapeDtypeStruct((blocks * PLANES, rows_out, depth), dtype),
+        in_specs=in_specs,
+        out_specs=block_spec,
+        out_shape=jax.ShapeDtypeStruct(shape, dtype),
         compiler_params=pltpu.CompilerParams(vmem_limit_bytes=VMEM_LIMIT),
         cost_estimate=pl.CostEstimate(
             flops=2 * blocks * PLANES * depth * matrix.size,
@@ -418,21 +411,16 @@
 
     start = (1 - place) * (half_rows - est_extra)
     edge = lax.dynamic_slice_in_dim(estimate, start, est_extra, 1)
-    edge = (edge - EST_MID).astype(BF16)
+    edge = lax.ppermute((edge - EST_MID).astype(BF16), "view", swap)
     centred = (estimate - EST_MID).astype(BF16)
-    inner_est = jnp.concatenate([centred, lax.ppermute(edge, "view", swap)], axis=1)
-    outer_est = jnp.concatenate(
-        [
-            lax.ppermute(inner_est[block - halo :], "tile", up),
-            lax.ppermute(inner_est[:halo], "tile", down),
-        ],
-        axis=0,
-    )
+    inner_est = jnp.concatenate([centred, edge], axis=1)
 
     other_start = (1 - place) * (half_rows - ROWS)
-    cuts = [0, (groups + 1) // 2, groups]
+    cuts = [0, groups - groups // 4, groups]
     arrived = []
     for low, high in zip(cuts, cuts[1:]):
+        if low > 0:
+            other_start, edge = lax.optimization_barrier((other_start, edge))
         piece = lax.dynamic_slice_in_dim(
             raw_tiles, other_start + low * ROWS, (high - low) * ROWS, 2
         )
@@ -442,6 +430,22 @@
     rounded = lax.reduce_precision(kernels, 8, 7)
     scale = 1.0 / jnp.prod(jnp.sum(rounded, axis=2), axis=1)
     position = jnp.stack([place, lax.axis_index("tile")]).astype(jnp.int32)
+
+    position, inner_est = lax.optimization_barrier((position, inner_est))
+    limits = depth_range.reshape(views * 2, 1).astype(BF16)
+    limits = jnp.pad(limits, ((0, inner_est.shape[1] - views * 2), (0, 0)))
+    limits = jnp.broadcast_to(limits[None], (1,) + inner_est.shape[1:])
+
+    def with_limits(planes):
+        return jnp.concatenate([planes, limits], axis=0)
+
+    from_below = lax.ppermute(with_limits(inner_est[block - halo :]), "tile", up)
+    from_above = lax.ppermute(with_limits(inner_est[:halo]), "tile", down)
+    outer_est = jnp.concatenate([from_below[:halo], from_above[:halo]], axis=0)
+    below, above = (
+        part[halo, : views * 2, 0].reshape(views, 1, 2).astype(jnp.int32)
+        for part in (from_below, from_above)
+    )
 
     smem = pl.BlockSpec(memory_space=pltpu.SMEM)
     vmem = pl.BlockSpec(memory_space=pltpu.VMEM)
@@ -466,8 +470,6 @@
         cost_estimate=pl.CostEstimate(flops=0, bytes_accessed=30_000_000, transcendentals=0),
     )(kernels, rounded, scale, view_offsets, depth_range, position)
 
-    below = lax.ppermute(depth_range, "tile", up)
-    above = lax.ppermute(depth_range, "tile", down)
     table_xz, table_y = pl.pallas_call(
         functools.partial(weight_tables_kernel, rows_all=rows_all),
         in_specs=[smem] * 6,
@@ -485,11 +487,13 @@
     own_first = lax.rem(place * slots + jnp.arange(views), views)
     starts = view_offsets[own_first, 0] + (halo - half)
     base = place * ((half_rows - ROWS) // ROWS)
+    base, table_xz, table_y = lax.optimization_barrier((base, table_xz, table_y))
     zero = jnp.zeros((), jnp.int32)
     parts = [
         view_pass(0, slots, 0, groups, base, starts[:slots], inner, outer, raw_tiles, tables)
     ]
     for low, high, piece in zip(cuts, cuts[1:], arrived):
+        zero, parts[-1] = lax.optimization_barrier((zero, parts[-1]))
         parts.append(
             view_pass(
                 1, slots, low, high - low, zero, starts[slots:], inner, outer, piece, tables
@@ -501,26 +505,16 @@
     edges = rows_back(
         parts, rows_mt, 2 * side, lambda i: jnp.where(i < side, i, i + middle), BF16
     )
-    kept = rows_back(parts, rows_mt, middle, lambda i: i + side, F32)
     low = lax.ppermute(edges[halo:], "tile", up)
     high = lax.ppermute(edges[:halo], "tile", down)
-    sides = halo // PLANES
-    whole = (PLANES, half_rows, depth)
-    return pl.pallas_call(
-        functools.partial(finish_kernel, sides=sides),
-        grid=(middle,),
-        in_specs=[
-            pl.BlockSpec(whole, lambda i: (i, 0, 0)),
-            pl.BlockSpec(whole, lambda i: (i, 0, 0)),
-            pl.BlockSpec(whole, lambda i: (jnp.minimum(i, sides - 1), 0, 0)),
-            pl.BlockSpec(whole, lambda i: (jnp.maximum(i - sides, 0), 0, 0)),
-            pl.BlockSpec(table_xz.shape, lambda i: (0, 0, 0)),
-            pl.BlockSpec(table_y.shape, lambda i: (0, 0, 0)),
-        ],
-        out_specs=pl.BlockSpec(whole, lambda i: (i, 0, 0)),
-        out_shape=jax.ShapeDtypeStruct(estimate.shape, F32),
-        compiler_params=pltpu.CompilerParams(vmem_limit_bytes=VMEM_LIMIT),
-    )(estimate, kept, low, high, table_xz, table_y)
+    kept = rows_back(parts, rows_mt, middle, lambda i: i + side, F32)
+    low = jnp.pad(low, ((0, block - halo), (0, 0), (0, 0))).astype(F32)
+    high = jnp.pad(high, ((block - halo, 0), (0, 0), (0, 0))).astype(F32)
+    weight = sum(
+        table_xz[view][:, None, :] * table_y[view][None, :, :1] for view in range(views)
+    )
+    correction = kept + low + high + QUO_MID * weight
+    return estimate * correction / jnp.maximum(weight, FLOOR)
 
 
 def solution(mesh):

time: 147 us -> 131 us (0.89)
  waiting for transfers between devices: 20.7 us -> 10.1 us
  Pallas kernels: 91.1 us -> 81.8 us
  other arithmetic: 3.04 us -> 11.9 us
  starting transfers between devices: 22 us -> 15.5 us
  local copies, waits for them, and re-layouts: 8.41 us -> 10.1 us
    ppermute x5 -> x3, waiting for transfers between devices: 20.7 us -> 0.01 us  [the longest x1 0.01 us: on_device(): edge = lax.ppermute((edge - EST_MID).astype(BF16), 'view', swap)]
    ppermute x1, waiting for transfers between devices: 0.01 us -> 8.68 us  [on_device(): low = lax.ppermute(edges[halo:], 'tile', up)]
    ppermute x5 -> x3, starting transfers between devices: 14.3 us -> 8.43 us  [the longest x1 4.44 us: on_device(): from_below = lax.ppermute(with_limits(inner_est[block - halo:]), 'tile', up)]
    pallas_call x3 -> x2, Pallas kernels: 17.5 us -> 11.8 us  [rows_back(): pl.pallas_call(rows_back_kernel, grid=(blocks,), in_specs=in_specs, out_s...]
    div x0 -> x1, other arithmetic: none -> 3.04 us  [on_device(): return estimate * correction / jnp.maximum(weight, FLOOR)]
    slice x1 -> x6, local copies, waits for them, and re-layouts: 0.1 us -> 2.99 us  [the longest x2 2.45 us: on_device(): outer_est = jnp.concatenate([from_below[:halo], from_above[:halo]], axis=0)]
    concatenate x3, other arithmetic: 0.41 us -> 3.23 us  [the longest x1 1.54 us: with_limits(): return jnp.concatenate([planes, limits], axis=0)]
    pallas_call x1, Pallas kernels: 15.2 us -> 12.7 us  [on_device(): pl.pallas_call(functools.partial(tables_kernel, slots=slots, tiles=tiles,...]
  transfers between devices with their start and end apart: 9 -> 7, of which waited for: 2 -> 2; matrix products, arithmetic and copies ran while one was open for 5% -> 13% of each run, Pallas kernels for 46% -> 54%
where the time goes in v4:
time: 131 us; the launch traced here: 130 us
  Pallas kernels  81.8 us (62%)
  starting transfers between devices  15.5 us (12%)
  other arithmetic  11.9 us (9%)
  local copies, waits for them, and re-layouts  10.1 us (8%)
  waiting for transfers between devices  10.1 us (8%)
    pallas_call x3, Pallas kernels, view_pass(): pl.pallas_call(view_kernel, grid_spec=pltpu.PrefetchScalarGridSpec(num_sc...  41.8 us
    pallas_call x1, Pallas kernels, on_device(): pl.pallas_call(functools.partial(tables_kernel, slots=slots, tiles=tiles,...  12.7 us
    pallas_call x2, Pallas kernels, rows_forward(): pl.pallas_call(rows_forward_kernel, grid=(count // PLANES,), in_specs=[pl...  12.4 us
    pallas_call x2, Pallas kernels, rows_back(): pl.pallas_call(rows_back_kernel, grid=(blocks,), in_specs=in_specs, out_s...  11.8 us
    ppermute x1, waiting for transfers between devices, on_device(): low = lax.ppermute(edges[halo:], 'tile', up)  8.68 us
    dynamic_slice x2, local copies, waits for them, and re-layouts, on_device(): lax.dynamic_slice_in_dim(raw_tiles, other_start + low * ROWS, (high - low...  5.67 us
    ppermute x1, starting transfers between devices, on_device(): from_below = lax.ppermute(with_limits(inner_est[block - halo:]), 'tile', up)  4.44 us
    ppermute x1, starting transfers between devices, on_device(): low = lax.ppermute(edges[halo:], 'tile', up)  3.92 us
  transfers between devices with their start and end apart: 7, of which 2 were waited for; matrix products, arithmetic and copies ran while one was open for 13% of the time, Pallas kernels for 54%

profile of v4, /device:TPU:1, one launch (start us, length us, event | category | flops | bytes accessed | tf_op | source)
XLA Modules:
  0.0 129.7 jit_solution(8328004530643286191)
XLA Ops:
  0.0 1.9 %add_convert_fusion.1 = bf16[24,32,128]{2,1,0:T(8,128)(2,1)} fusion(f32[24,256,128]{2,1,0:T(8,128)} %param.5, s32[]{:T(128)S(6)} %select_n.19), kind=kLoop, calls=%fused_computation.7 | loop fusion | flops 196608 | bytes 589828 | tf_op jit(solution)/shard_map/convert_element_type | solution.py:414
  1.9 2.1 %collective-permute-start = (bf16[24,32,128]{2,1,0:T(8,128)(2,1)}, bf16[24,32,128]{2,1,0:T(8,128)(2,1)S(1)}, u32[]{:S(2)}, u32[]{:S(2)}) collective-permute-start(bf16[24,32,128]{2,1,0:T(8,128)(2,1)} %add_convert_fusion.1), channel_id=1, source_target_pairs={{0,16},{16,0},{1,17},{17,1},{2,18},{18,2},{3,19},{19,3},{4,20},{20... | collective-permute-start | bytes 589832 | tf_op jit(solution)/shard_map/ppermute | solution.py:414
  3.9 3.4 %constant_dynamic-slice_fusion = bf16[2,24,208,128]{3,2,1,0:T(8,128)(2,1)} fusion(bf16[2,24,512,128]{3,2,1,0:T(8,128)(2,1)} %raw_ref.1, s32[]{:T(128)S(6)} %select_n.21), kind=kLoop, calls=%fused_computation.27 | loop fusion | bytes 5111812 | tf_op jit(solution)/shard_map/dynamic_slice | solution.py:424
  7.3 1.5 %add_convert_fusion = bf16[24,256,128]{2,1,0:T(8,128)(2,1)} fusion(f32[24,256,128]{2,1,0:T(8,128)S(1)} %copy-done.9), kind=kLoop, calls=%fused_computation.2 | loop fusion | flops 1572864 | bytes 4718592 | tf_op jit(solution)/shard_map/convert_element_type | solution.py:415
  9.3 0.6 gather_fusion
  10.0 0.2 reduce-precision_reduce_fusion
  10.2 1.5 %pad_maximum_fusion.est_ref = bf16[24,288,128]{2,1,0:T(8,128)(2,1)S(1)} fusion(bf16[24,32,128]{2,1,0:T(8,128)(2,1)S(1)} %collective-permute-done, bf16[24,256,128]{2,1,0:T(8,128)(2,1)} %add_convert_fusion), kind=kLoop, calls=%fused_computation.3 | loop fusion | flops 3538944 | bytes 3538944 | tf_op jit(solution)/shard_map/concatenate | solution.py:416
  12.0 1.5 %pad_maximum_fusion.2 = (bf16[13,288,128]{2,1,0:T(8,128)(2,1)}, bf16[13,288,128]{2,1,0:T(8,128)(2,1)}) fusion(bf16[1,288,128]{2,1,0:T(8,128)(2,1)S(1)} %broadcast_in_dim.11, bf16[12,288,128]{2,1,0:T(8,128)(2,1)S(1)} %get-tuple-element.51, bf16[12,288,128]{2,1,0:T(8,128)(2,1)S(1)} %get-tuple-element.52), kind=kLoop, calls=%fused_computation.5 | loop fusion | flops 958464 | bytes 3760128 | tf_op jit(solution)/shard_map/concatenate | solution.py:440
  13.5 4.4 %collective-permute-start.1 = (bf16[13,288,128]{2,1,0:T(8,128)(2,1)}, bf16[13,288,128]{2,1,0:T(8,128)(2,1)}, u32[]{:S(2)}, u32[]{:S(2)}) collective-permute-start(bf16[13,288,128]{2,1,0:T(8,128)(2,1)} %get-tuple-element.60), channel_id=1, source_target_pairs={{0,1},{1,2},{2,3},{3,4},{4,5},{5,6},{6,7},{7,8},{8,9},{9,10},{10,1... | collective-permute-start | bytes 2875400 | tf_op jit(solution)/shard_map/ppermute | solution.py:442
  18.0 1.9 %collective-permute-start.2 = (bf16[13,288,128]{2,1,0:T(8,128)(2,1)}, bf16[13,288,128]{2,1,0:T(8,128)(2,1)}, u32[]{:S(2)}, u32[]{:S(2)}) collective-permute-start(bf16[13,288,128]{2,1,0:T(8,128)(2,1)} %get-tuple-element.59), channel_id=1, source_target_pairs={{1,0},{2,1},{3,2},{4,3},{5,4},{6,5},{7,6},{8,7},{9,8},{10,9},{11,1... | collective-permute-start | bytes 2875400 | tf_op jit(solution)/shard_map/ppermute | solution.py:443
  20.2 2.3 %constant_dynamic-slice_fusion.1 = bf16[2,24,64,128]{3,2,1,0:T(8,128)(2,1)} fusion(bf16[2,24,512,128]{3,2,1,0:T(8,128)(2,1)} %raw_ref.1, s32[]{:T(128)S(6)} %select_n.22), kind=kLoop, calls=%fused_computation.28 | loop fusion | bytes 1572868 | tf_op jit(solution)/shard_map/dynamic_slice | solution.py:424
  22.5 1.3 collective-permute-start.4
  23.8 12.7 %shard_map.56 = (bf16[1088,288]{1,0:T(8,128)(2,1)S(1)}, bf16[256,1088]{1,0:T(8,128)(2,1)S(1)}, bf16[4,192,320]{2,1,0:T(8,128)(2,1)S(1)}, bf16[4,320,192]{2,1,0:T...) custom-call(f32[4,3,17]{2,1,0:T(4,128)S(1)} %get-tuple-element.50.ex, ...), custom_call_target="tpu_custom_call" | custom-call | bytes 30000000 | tf_op jit(solution)/shard_map/pallas_call | solution.py:464
  36.5 6.2 %shard_map.57.inner_ref = bf16[4,17,24,16,128]{4,3,2,1,0:T(8,128)(2,1)} custom-call(bf16[24,288,128]{2,1,0:T(8,128)(2,1)S(1)} %pad_maximum_fusion.est_ref, bf16[1088,288]{1,0:T(8,128)(2,1)S(1)} %get-tuple-element.32.matrix_ref), custom_call_target="tpu_custom_call" | custom-call | flops 1925185536 | bytes 8454144 | tf_op jit(solution)/shard_map/pallas_call | solution.py:205
  42.7 0.8 convert_reduce_fusion.1
  43.6 0.7 convert_reduce_fusion
  44.4 3.2 %shard_map.55 = (f32[4,24,128]{2,1,0:T(8,128)S(1)}, f32[4,256,128]{2,1,0:T(8,128)S(1)}) custom-call(f32[4,3,17]{2,1,0:T(4,128)S(1)} %get-tuple-element.50.exact_ref, s32[4,3]{1,0:T(4,128)S(1)} %copy-done, s32[4,1,2]{2,1,0:T(1,128)S(1)} %bitcast.27, s32[4,1,2]{2,1,0:T(1,128)S(1)} %copy.29.range_ref, s32[4,1,2]{2,1,0:T(1,128)S(1)} %bitcast.28, ...), custom_call_target="tpu_custom_call" | custom-call | bytes 8000000 | tf_op jit(solution)/shard_map/pallas_call | solution.py:473
  47.6 1.2 slice.94
  48.8 1.2 slice.93
  50.2 0.2 pad_maximum_fusion.1.est_ref
  50.4 6.2 %shard_map.58.outer_ref = bf16[4,17,24,16,128]{4,3,2,1,0:T(8,128)(2,1)} custom-call(bf16[24,288,128]{2,1,0:T(8,128)(2,1)S(1)} %pad_maximum_fusion.1.est_ref, bf16[1088,288]{1,0:T(8,128)(2,1)S(1)} %get-tuple-element.32.matrix_ref), custom_call_target="tpu_custom_call" | custom-call | flops 1925185536 | bytes 8454144 | tf_op jit(solution)/shard_map/pallas_call | solution.py:205
  56.6 20.3 %shard_map.59.refs_0_ = bf16[2,17,48,16,128]{4,3,2,1,0:T(8,128)(2,1)} custom-call(s32[3]{0:T(128)S(1)} %pad_add_fusion.1.scalar_ref, bf16[4,17,24,16,128]{4,3,2,1,0:T(8,128)(2,1)} %shard_map.57.inner_ref, bf16[4,17,24,16,128]{4,3,2,1,0:T(8,128)(2,1)} %shard_map.58.outer_ref, bf16[2,24,512,128]{3,2,1,0:T(8,128)(2,1)} %raw_ref.1, ...), custom_call_target="tpu_custom_call" | custom-call | flops 13369344000 | bytes 16711680 | tf_op jit(solution)/shard_map/pallas_call | solution.py:309
  76.9 16.0 %shard_map.60.refs_1_ = bf16[2,13,48,16,128]{4,3,2,1,0:T(8,128)(2,1)} custom-call(s32[3]{0:T(128)S(1)} %pad_add_fusion.2.scalar_ref, bf16[4,17,24,16,128]{4,3,2,1,0:T(8,128)(2,1)} %shard_map.57.inner_ref, bf16[4,17,24,16,128]{4,3,2,1,0:T(8,128)(2,1)} %shard_map.58.outer_ref, bf16[2,24,208,128]{3,2,1,0:T(8,128)(2,1)} %collective-permute-done.3.raw_ref, ...), custom_call_target="tpu_custom_call" | custom-call | flops 10223616000 | bytes 12779520 | tf_op jit(solution)/shard_map/pallas_call | solution.py:309
  93.0 5.5 %shard_map.61.refs_2_ = bf16[2,4,48,16,128]{4,3,2,1,0:T(8,128)(2,1)S(1)} custom-call(s32[3]{0:T(128)S(1)} %pad_add_fusion.3.scalar_ref, bf16[4,17,24,16,128]{4,3,2,1,0:T(8,128)(2,1)} %shard_map.57.inner_ref, bf16[4,17,24,16,128]{4,3,2,1,0:T(8,128)(2,1)} %shard_map.58.outer_ref, bf16[2,24,64,128]{3,2,1,0:T(8,128)(2,1)} %collective-permute-done.4.raw_ref, ...), custom_call_target="tpu_custom_call" | custom-call | flops 3145728000 | bytes 3932160 | tf_op jit(solution)/shard_map/pallas_call | solution.py:309
  98.5 5.8 %shard_map.63 = bf16[24,256,128]{2,1,0:T(8,128)(2,1)S(1)} custom-call(bf16[2,17,48,16,128]{4,3,2,1,0:T(8,128)(2,1)} %shard_map.59.refs_0_, bf16[2,13,48,16,128]{4,3,2,1,0:T(8,128)(2,1)} %shard_map.60.refs_1_, bf16[2,4,48,16,128]{4,3,2,1,0:T(8,128)(2,1)S(1)} %shard_map.61.refs_2_, bf16[256,1088]{1,0:T(8,128)(2,1)S(1)} %get-tuple-element.46.refs_3_), custom_call_target="tpu_custom_call" | custom-call | flops 1711276032 | bytes 9830400 | tf_op jit(solution)/shard_map/pallas_call | solution.py:380
  104.4 1.9 %collective-permute-start.6 = (bf16[12,256,128]{2,1,0:T(8,128)(2,1)S(1)}, bf16[12,256,128]{2,1,0:T(8,128)(2,1)S(1)}, u32[]{:S(2)}, u32[]{:S(2)}) collective-permute-start(bf16[12,256,128]{2,1,0:T(8,128)(2,1)S(1)} %get-tuple-element.54), channel_id=1, source_target_pairs={{1,0},{2,1},{3,2},{4,3},{5,4},{6,5},{7,6},{8,7},{9,8},{10,9},{11,1... | collective-permute-start | bytes 2359304 | tf_op jit(solution)/shard_map/ppermute | solution.py:509
  106.4 3.9 %collective-permute-start.5 = (bf16[12,256,128]{2,1,0:T(8,128)(2,1)S(1)}, bf16[12,256,128]{2,1,0:T(8,128)(2,1)S(1)}, u32[]{:S(2)}, u32[]{:S(2)}) collective-permute-start(bf16[12,256,128]{2,1,0:T(8,128)(2,1)S(1)} %get-tuple-element.53), channel_id=1, source_target_pairs={{0,1},{1,2},{2,3},{3,4},{4,5},{5,6},{6,7},{7,8},{8,9},{9,10},{10,1... | collective-permute-start | bytes 2359304 | tf_op jit(solution)/shard_map/ppermute | solution.py:508
  110.5 0.2 slice_reduce_fusion.2
  110.6 5.9 %shard_map.62 = f32[24,256,128]{2,1,0:T(8,128)S(1)} custom-call(bf16[2,17,48,16,128]{4,3,2,1,0:T(8,128)(2,1)} %shard_map.59.refs_0_, bf16[2,13,48,16,128]{4,3,2,1,0:T(8,128)(2,1)} %shard_map.60.refs_1_, bf16[2,4,48,16,128]{4,3,2,1,0:T(8,128)(2,1)S(1)} %shard_map.61.refs_2_, bf16[256,1088]{1,0:T(8,128)(2,1)S(1)} %get-tuple-element.46.refs_3_), custom_call_target="tpu_custom_call" | custom-call | flops 1711276032 | bytes 9830400 | tf_op jit(solution)/shard_map/pallas_call | solution.py:380
  116.6 1.4 %collective-permute-done.6 = bf16[12,256,128]{2,1,0:T(8,128)(2,1)S(1)} collective-permute-done((bf16[12,256,128]{2,1,0:T(8,128)(2,1)S(1)}, bf16[12,256,128]{2,1,0:T(8,128)(2,1)S(1)}, u32[]{:S(2)}, u32[]{:S(2)}) %collective-permute-start.6) | collective-permute-done | bytes 786464 | tf_op jit(solution)/shard_map/ppermute | solution.py:509
  118.0 8.7 %collective-permute-done.5 = bf16[12,256,128]{2,1,0:T(8,128)(2,1)S(1)} collective-permute-done((bf16[12,256,128]{2,1,0:T(8,128)(2,1)S(1)}, bf16[12,256,128]{2,1,0:T(8,128)(2,1)S(1)}, u32[]{:S(2)}, u32[]{:S(2)}) %collective-permute-start.5) | collective-permute-done | bytes 786464 | tf_op jit(solution)/shard_map/ppermute | solution.py:508
  126.7 3.0 %maximum_divide_fusion = f32[24,256,128]{2,1,0:T(8,128)} fusion(f32[24,256,128]{2,1,0:T(8,128)S(1)} %copy-done.10, f32[24,256,128]{2,1,0:T(8,128)S(1)} %shard_map.62, f32[256]{0:T(256)S(1)} %get-tuple-element.67, f32[24,128]{1,0:T(8,128)S(1)} %get-tuple-element.62, f32[256]{0:T(256)S(1)} %get-tuple-element.68, f32[24,128]{1,0:T(8,128)S(1)} %get-tuple-element.63, ...), kind=kLoop, calls=%fused_computation.1 | loop fusion | flops 12582912 | bytes 11063296 | tf_op jit(solution)/shard_map/div | solution.py:517
  (57 shorter events, 1.8 us)
Async XLA Ops:
  0.0 7.3 %copy-start.9 = (f32[24,256,128]{2,1,0:T(8,128)S(1)}, f32[24,256,128]{2,1,0:T(8,128)}, u32[]{:S(2)}) copy-start(f32[24,256,128]{2,1,0:T(8,128)} %param.5) | copy-start | bytes 9437188
  1.9 8.3 %collective-permute-start = (bf16[24,32,128]{2,1,0:T(8,128)(2,1)}, bf16[24,32,128]{2,1,0:T(8,128)(2,1)S(1)}, u32[]{:S(2)}, u32[]{:S(2)}) collective-permute-start(bf16[24,32,128]{2,1,0:T(8,128)(2,1)} %add_convert_fusion.1), channel_id=1, source_target_pairs={{0,16},{16,0},{1,17},{17,1},{2,18},{18,2},{3,19},{19,3},{4,20},{20... | collective-permute-start | bytes 589832 | tf_op jit(solution)/shard_map/ppermute | solution.py:414
  7.3 1.6 %copy-start.11 = (f32[4,3,17]{2,0,1:T(4,128)S(1)}, f32[4,3,17]{2,0,1:T(4,128)}, u32[]{:S(2)}) copy-start(f32[4,3,17]{2,0,1:T(4,128)} %param.7) | copy-start | bytes 2452
  7.3 1.8 %copy-start.12 = (s32[4,1,2]{0,2,1:T(2,128)S(1)}, s32[4,1,2]{0,2,1:T(2,128)}, u32[]{:S(2)}) copy-start(s32[4,1,2]{0,2,1:T(2,128)} %param.9) | copy-start | bytes 100
  7.3 2.0 %copy-start = (s32[4,3]{1,0:T(4,128)S(1)}, s32[4,3]{1,0:T(4,128)}, u32[]{:S(2)}) copy-start(s32[4,3]{1,0:T(4,128)} %offset_ref.3) | copy-start | bytes 148
  7.3 69.6 %collective-permute-start.3 = (bf16[2,24,208,128]{3,2,1,0:T(8,128)(2,1)}, bf16[2,24,208,128]{3,2,1,0:T(8,128)(2,1)}, u32[]{:S(2)}, u32[]{:S(2)}) collective-permute-start(bf16[2,24,208,128]{3,2,1,0:T(8,128)(2,1)} %constant_dynamic-slice_fusion), channel_id=1, source_target_pairs={{0,16},{16,0},{1,17},{17,1},{2,18},{18,2},{3,19},{19,3},{4,20},{20... | collective-permute-start | bytes 7667720 | tf_op jit(solution)/shard_map/ppermute | solution.py:427
  13.5 29.2 %collective-permute-start.1 = (bf16[13,288,128]{2,1,0:T(8,128)(2,1)}, bf16[13,288,128]{2,1,0:T(8,128)(2,1)}, u32[]{:S(2)}, u32[]{:S(2)}) collective-permute-start(bf16[13,288,128]{2,1,0:T(8,128)(2,1)} %get-tuple-element.60), channel_id=1, source_target_pairs={{0,1},{1,2},{2,3},{3,4},{4,5},{5,6},{6,7},{7,8},{8,9},{9,10},{10,1... | collective-permute-start | bytes 2875400 | tf_op jit(solution)/shard_map/ppermute | solution.py:442
  18.0 25.6 %collective-permute-start.2 = (bf16[13,288,128]{2,1,0:T(8,128)(2,1)}, bf16[13,288,128]{2,1,0:T(8,128)(2,1)}, u32[]{:S(2)}, u32[]{:S(2)}) collective-permute-start(bf16[13,288,128]{2,1,0:T(8,128)(2,1)} %get-tuple-element.59), channel_id=1, source_target_pairs={{1,0},{2,1},{3,2},{4,3},{5,4},{6,5},{7,6},{8,7},{9,8},{10,9},{11,1... | collective-permute-start | bytes 2875400 | tf_op jit(solution)/shard_map/ppermute | solution.py:443
  22.5 70.5 %collective-permute-start.4 = (bf16[2,24,64,128]{3,2,1,0:T(8,128)(2,1)}, bf16[2,24,64,128]{3,2,1,0:T(8,128)(2,1)}, u32[]{:S(2)}, u32[]{:S(2)}) collective-permute-start(bf16[2,24,64,128]{3,2,1,0:T(8,128)(2,1)} %constant_dynamic-slice_fusion.1), channel_id=1, source_target_pairs={{0,16},{16,0},{1,17},{17,1},{2,18},{18,2},{3,19},{19,3},{4,20},{20... | collective-permute-start | bytes 2359304 | tf_op jit(solution)/shard_map/ppermute | solution.py:427
  36.4 6.3 %copy-start.1 = (bf16[4,320,192]{2,1,0:T(8,128)(2,1)}, bf16[4,320,192]{2,1,0:T(8,128)(2,1)S(1)}, u32[]{:S(2)}) copy-start(bf16[4,320,192]{2,1,0:T(8,128)(2,1)S(1)} %get-tuple-element.34.plane_t_ref) | copy-start | bytes 1474564
  36.4 6.2 %copy-start.3 = (bf16[4,192,320]{2,1,0:T(8,128)(2,1)}, bf16[4,192,320]{2,1,0:T(8,128)(2,1)S(1)}, u32[]{:S(2)}) copy-start(bf16[4,192,320]{2,1,0:T(8,128)(2,1)S(1)} %get-tuple-element.33.plane_ref) | copy-start | bytes 1474564
  36.4 6.2 %copy-start.5 = (f32[4,272,128]{2,1,0:T(8,128)}, f32[4,272,128]{2,1,0:T(8,128)S(1)}, u32[]{:S(2)}) copy-start(f32[4,272,128]{2,1,0:T(8,128)S(1)} %get-tuple-element.38.ones_yz_ref) | copy-start | bytes 1671172
  36.5 6.2 %copy-start.7 = (f32[4,24,8,128]{3,2,1,0:T(8,128)}, f32[4,24,8,128]{3,2,1,0:T(8,128)S(1)}, u32[]{:S(2)}) copy-start(f32[4,24,8,128]{3,2,1,0:T(8,128)S(1)} %get-tuple-element.37.ones_x_ref) | copy-start | bytes 1179652
  50.3 6.2 %copy-start.2 = (bf16[4,320,192]{2,1,0:T(8,128)(2,1)S(1)}, bf16[4,320,192]{2,1,0:T(8,128)(2,1)}, u32[]{:S(2)}) copy-start(bf16[4,320,192]{2,1,0:T(8,128)(2,1)} %copy-done.1) | copy-start | bytes 1474564
  50.3 6.2 %copy-start.4 = (bf16[4,192,320]{2,1,0:T(8,128)(2,1)S(1)}, bf16[4,192,320]{2,1,0:T(8,128)(2,1)}, u32[]{:S(2)}) copy-start(bf16[4,192,320]{2,1,0:T(8,128)(2,1)} %copy-done.3) | copy-start | bytes 1474564
  50.3 6.2 %copy-start.6 = (f32[4,272,128]{2,1,0:T(8,128)S(1)}, f32[4,272,128]{2,1,0:T(8,128)}, u32[]{:S(2)}) copy-start(f32[4,272,128]{2,1,0:T(8,128)} %copy-done.5) | copy-start | bytes 1671172
  50.3 6.2 %copy-start.8 = (f32[4,24,8,128]{3,2,1,0:T(8,128)S(1)}, f32[4,24,8,128]{3,2,1,0:T(8,128)}, u32[]{:S(2)}) copy-start(f32[4,24,8,128]{3,2,1,0:T(8,128)} %copy-done.7) | copy-start | bytes 1179652
  104.4 13.6 %collective-permute-start.6 = (bf16[12,256,128]{2,1,0:T(8,128)(2,1)S(1)}, bf16[12,256,128]{2,1,0:T(8,128)(2,1)S(1)}, u32[]{:S(2)}, u32[]{:S(2)}) collective-permute-start(bf16[12,256,128]{2,1,0:T(8,128)(2,1)S(1)} %get-tuple-element.54), channel_id=1, source_target_pairs={{1,0},{2,1},{3,2},{4,3},{5,4},{6,5},{7,6},{8,7},{9,8},{10,9},{11,1... | collective-permute-start | bytes 2359304 | tf_op jit(solution)/shard_map/ppermute | solution.py:509
  106.4 20.3 %collective-permute-start.5 = (bf16[12,256,128]{2,1,0:T(8,128)(2,1)S(1)}, bf16[12,256,128]{2,1,0:T(8,128)(2,1)S(1)}, u32[]{:S(2)}, u32[]{:S(2)}) collective-permute-start(bf16[12,256,128]{2,1,0:T(8,128)(2,1)S(1)} %get-tuple-element.53), channel_id=1, source_target_pairs={{0,1},{1,2},{2,3},{3,4},{4,5},{5,6},{6,7},{7,8},{8,9},{9,10},{10,1... | collective-permute-start | bytes 2359304 | tf_op jit(solution)/shard_map/ppermute | solution.py:508
  110.6 16.1 %copy-start.10 = (f32[24,256,128]{2,1,0:T(8,128)S(1)}, f32[24,256,128]{2,1,0:T(8,128)}, u32[]{:S(2)}) copy-start(f32[24,256,128]{2,1,0:T(8,128)} %param.5) | copy-start | bytes 9437188
